TPU v7x, 32 devices: a whole 2x2x4 slice. The times are simulated.
32 devices in a mesh: dp: 8 (over z, y), mp: 4 (over x, core).
Axes of the slice: x: 2, y: 2, z: 4, core: 2. Of those that a mesh axis runs over, the one named last changes fastest.
Arguments:
- block_input: bfloat16 [8192, 1024], P('dp')
- out_cotangent: bfloat16 [8192, 1024], P('dp')
- sigmas: float32 [32], replicated, may hold values from 0.02 to 80
- class_labels: int32 [32], replicated, may hold values from 0 to 999
- image_lengths: int32 [32], replicated, may hold values from 0 to 1024, as said below
- fourier_freqs: float32 [384], replicated, may hold values from -4 to 4
- inproj_state: float32 [4, 1024, 3, 1024], P(None, 'dp', None, 'mp'), as said below
- outproj_state: float32 [4, 1024, 1024], P(None, 'mp', 'dp'), as said below
- upproj_state: float32 [4, 1024, 2, 3072], P(None, 'dp', None, 'mp'), as said below
- downproj_state: float32 [4, 3072, 1024], P(None, 'mp', 'dp'), as said below
- timeproj_state: float32 [4, 768, 768], P(None, 'dp'), as said below
- classemb_state: float32 [4, 1000, 768], P(None, None, 'dp'), as said below
- mapup_state: float32 [4, 768, 2, 2304], P(None, 'dp', None, 'mp'), as said below
- mapdown_state: float32 [4, 2304, 768], P(None, 'mp', 'dp'), as said below
- modproj_state: float32 [4, 768, 2, 1024], P(None, 'dp'), as said below
- gains_state: float32 [4, 3, 768], P(None, None, 'dp'), as said below
- headscale_state: float32 [4, 16], P(None, 'mp'), as said below
Outputs:
- layer_out: bfloat16 [8192, 1024], P('dp')
- input_grad: float32 [8192, 1024], P('dp')
- grad_norm: float32 [], replicated
- new_inproj: float32 [2, 1024, 3, 1024], P(None, 'dp', None, 'mp')
- inproj_first: float32 [1024, 3, 1024], P('dp', None, 'mp')
- inproj_second: float32 [1024, 3, 1024], P('dp', None, 'mp')
- new_outproj: float32 [2, 1024, 1024], P(None, 'mp', 'dp')
- outproj_first: float32 [1024, 1024], P('mp', 'dp')
- outproj_second: float32 [1024, 1024], P('mp', 'dp')
- new_upproj: float32 [2, 1024, 2, 3072], P(None, 'dp', None, 'mp')
- upproj_first: float32 [1024, 2, 3072], P('dp', None, 'mp')
- upproj_second: float32 [1024, 2, 3072], P('dp', None, 'mp')
- new_downproj: float32 [2, 3072, 1024], P(None, 'mp', 'dp')
- downproj_first: float32 [3072, 1024], P('mp', 'dp')
- downproj_second: float32 [3072, 1024], P('mp', 'dp')
- new_timeproj: float32 [2, 768, 768], P(None, 'dp')
- timeproj_first: float32 [768, 768], P('dp')
- timeproj_second: float32 [768, 768], P('dp')
- new_classemb: float32 [2, 1000, 768], P(None, None, 'dp')
- classemb_first: float32 [1000, 768], P(None, 'dp')
- classemb_second: float32 [1000, 768], P(None, 'dp')
- new_mapup: float32 [2, 768, 2, 2304], P(None, 'dp', None, 'mp')
- mapup_first: float32 [768, 2, 2304], P('dp', None, 'mp')
- mapup_second: float32 [768, 2, 2304], P('dp', None, 'mp')
- new_mapdown: float32 [2, 2304, 768], P(None, 'mp', 'dp')
- mapdown_first: float32 [2304, 768], P('mp', 'dp')
- mapdown_second: float32 [2304, 768], P('mp', 'dp')
- new_modproj: float32 [2, 768, 2, 1024], P(None, 'dp')
- modproj_first: float32 [768, 2, 1024], P('dp')
- modproj_second: float32 [768, 2, 1024], P('dp')
- new_gains: float32 [2, 3, 768], P(None, None, 'dp')
- gains_first: float32 [3, 768], P(None, 'dp')
- gains_second: float32 [3, 768], P(None, 'dp')
- new_headscale: float32 [2, 16], P(None, 'mp')
- headscale_first: float32 [16], P('mp')
- headscale_second: float32 [16], P('mp')
Inputs may be any that keep to these rules, and one draw needn't show every extreme that they name: `image_lengths`: each data shard's 4 entries are either 1024 followed by zeros, or k >= 1 entries of 256 followed by zeros; in every draw some shard holds one image of 1024 tokens and another holds 4 images of 256. `inproj_state`: second moments are positive. `outproj_state`: second moments are positive. `upproj_state`: second moments are positive. `downproj_state`: second moments are positive. `timeproj_state`: second moments are positive. `classemb_state`: second moments are positive. `mapup_state`: second moments are positive. `mapdown_state`: second moments are positive. `modproj_state`: second moments are positive. `gains_state`: second moments are positive. `headscale_state`: second moments and scales are positive.
All inputs are finite; a program needn't handle non-finite values.
Results may differ from a plain program's by a relative error of at most 0.02.
The roundings to bfloat16 on the way count: a program that leaves them out, or rounds other values in their place, can miss the bound.
Values may be sent and summed in bfloat16 or wider, within the bound.
A program may use at most 256 MiB of HBM per device.

v0:
```python
import math

import jax
import jax.numpy as jnp
from jax import lax
from jax.sharding import PartitionSpec as P

D = 1024
H = 16
FF = 3072
DM = 768
MFF = 2304
NCLASS = 1000
IMG_DEV = 4
STEP = 10


EPSILON = 1e-06
HIGHEST = lax.Precision.HIGHEST
BETA_ONE = 0.9
BETA_TWO = 0.95
ADAM_EPSILON = 1e-08
CLIP_NORM = 1.0
MASKED = -1e30


def rms_scale(values, scales):
    return values * lax.rsqrt(jnp.mean(values * values, axis=-1, keepdims=True) + EPSILON) * scales


def geglu_gate(hidden):
    return hidden[:, 0] * jax.nn.gelu(hidden[:, 1], approximate=False)


def fourier(sigmas, fourier_freqs):
    angles = 2.0 * math.pi * (jnp.log(sigmas) / 4.0)[:, None] * fourier_freqs[None, :]
    return jnp.concatenate([jnp.cos(angles), jnp.sin(angles)], axis=1)


def cosine(queries, key_rows, head_scale):
    query_unit = (
        queries
        * lax.rsqrt(jnp.sum(queries * queries, axis=-1, keepdims=True) + EPSILON)
        * head_scale[None, :, None]
    )
    key_unit = key_rows * lax.rsqrt(jnp.sum(key_rows * key_rows, axis=-1, keepdims=True) + EPSILON)
    return (query_unit, key_unit)


def learn_rates():
    return (
        2.5 * D ** (-0.5),
        2.5 * (D // 64) ** (-0.5),
        2.5 * D ** (-0.5),
        2.5 * FF ** (-0.5),
        2.5 * DM ** (-0.5),
        2.5,
        2.5 * DM ** (-0.5),
        2.5 * MFF ** (-0.5),
        1.25 * DM ** (-0.5),
        0.25,
        7.5,
    )


def decay_rates():
    return (0.01, 0.01, 0.01, 0.01, 0.01, 0.01, 0.01, 0.01, 0.01, 0.0, 0.0)


def adamw_step(state, gradient, rate, decay):
    keep_rate = 1.0 - (1.0 + STEP) ** (-0.75)
    first = BETA_ONE * state[1] + (1.0 - BETA_ONE) * gradient
    second = BETA_TWO * state[2] + (1.0 - BETA_TWO) * gradient * gradient
    first_hat = first / (1.0 - BETA_ONE**STEP)
    second_hat = second / (1.0 - BETA_TWO**STEP)
    weight = state[0] * (1.0 - rate * decay) - rate * first_hat / (
        jnp.sqrt(second_hat) + ADAM_EPSILON
    )
    average = keep_rate * state[3] + (1.0 - keep_rate) * weight
    return (jnp.stack([weight, average]), first, second)


def map_forward(
    feats_low, onehot_low, w_time, w_class, gain_values, w_mapup, w_mapdown, w_mod, reduce_sum
):
    embedded = jnp.dot(feats_low, w_time, preferred_element_type=jnp.float32) + jnp.dot(
        onehot_low, w_class, preferred_element_type=jnp.float32
    )
    unit_rms, unit_back = jax.vjp(rms_scale, embedded, gain_values[0])
    pre_up, pre_back = jax.vjp(rms_scale, unit_rms, gain_values[1])
    pre_low = pre_up.astype(jnp.bfloat16)
    map_hidden = jnp.einsum("id,dcf->icf", pre_low, w_mapup, preferred_element_type=jnp.float32)
    map_gated, gate_back = jax.vjp(geglu_gate, map_hidden)
    gated_low = map_gated.astype(jnp.bfloat16)
    mixed = unit_rms + reduce_sum(jnp.dot(gated_low, w_mapdown, preferred_element_type=jnp.float32))
    cond_vals, cond_back = jax.vjp(rms_scale, mixed, gain_values[2])
    cond_low = cond_vals.astype(jnp.bfloat16)
    modulation = jnp.einsum("id,dcf->icf", cond_low, w_mod, preferred_element_type=jnp.float32)
    return (modulation, (unit_back, pre_back, pre_low, gate_back, gated_low, cond_back, cond_low))


def map_backward(kept_items, grad_mods, feats_low, w_mapup, w_mapdown, w_mod, reduce_sum):
    unit_back, pre_back, pre_low, gate_back, gated_low, cond_back, cond_low = kept_items
    grad_cond = jnp.einsum("icf,dcf->id", grad_mods, w_mod.astype(jnp.float32), precision=HIGHEST)
    grad_mod = jnp.einsum("id,icf->dcf", cond_low.astype(jnp.float32), grad_mods, precision=HIGHEST)
    grad_mixed, grad_gain_two = cond_back(grad_cond)
    grad_mapdown = jnp.dot(gated_low.astype(jnp.float32).T, grad_mixed, precision=HIGHEST)
    (grad_hidden,) = gate_back(
        jnp.dot(grad_mixed, w_mapdown.astype(jnp.float32).T, precision=HIGHEST)
    )
    grad_mapup = jnp.einsum(
        "id,icf->dcf", pre_low.astype(jnp.float32), grad_hidden, precision=HIGHEST
    )
    grad_pre = reduce_sum(
        jnp.einsum("icf,dcf->id", grad_hidden, w_mapup.astype(jnp.float32), precision=HIGHEST)
    )
    grad_unit, grad_gain_one = pre_back(grad_pre)
    grad_embedded, grad_gain_zero = unit_back(grad_mixed + grad_unit)
    grad_time = jnp.dot(feats_low.astype(jnp.float32).T, grad_embedded, precision=HIGHEST)
    grad_gains = jnp.stack([grad_gain_zero, grad_gain_one, grad_gain_two])
    return (grad_embedded, grad_time, grad_mapup, grad_mapdown, grad_mod, grad_gains)


def per_device(
    block_input,
    out_cotangent,
    sigmas,
    class_labels,
    image_lengths,
    fourier_freqs,
    inproj_state,
    outproj_state,
    upproj_state,
    downproj_state,
    timeproj_state,
    classemb_state,
    mapup_state,
    mapdown_state,
    modproj_state,
    gains_state,
    headscale_state,
):
    shard_index = lax.axis_index("dp")
    tensor_index = lax.axis_index("mp")
    tensor_count = lax.axis_size("mp")
    image_start = shard_index * IMG_DEV
    my_sigmas = lax.dynamic_slice_in_dim(sigmas, image_start, IMG_DEV)
    my_classes = lax.dynamic_slice_in_dim(class_labels, image_start, IMG_DEV)
    my_lengths = lax.dynamic_slice_in_dim(image_lengths, image_start, IMG_DEV)
    gathered = (
        lax.all_gather(inproj_state[0].astype(jnp.bfloat16), "dp", axis=0, tiled=True),
        lax.all_gather(outproj_state[0].astype(jnp.bfloat16), "dp", axis=1, tiled=True),
        lax.all_gather(upproj_state[0].astype(jnp.bfloat16), "dp", axis=0, tiled=True),
        lax.all_gather(downproj_state[0].astype(jnp.bfloat16), "dp", axis=1, tiled=True),
        lax.all_gather(timeproj_state[0].astype(jnp.bfloat16), "dp", axis=0, tiled=True),
        lax.all_gather(classemb_state[0].astype(jnp.bfloat16), "dp", axis=1, tiled=True),
        lax.all_gather(mapup_state[0].astype(jnp.bfloat16), "dp", axis=0, tiled=True),
        lax.all_gather(mapdown_state[0].astype(jnp.bfloat16), "dp", axis=1, tiled=True),
        lax.all_gather(modproj_state[0].astype(jnp.bfloat16), "dp", axis=0, tiled=True),
        lax.all_gather(gains_state[0].astype(jnp.bfloat16), "dp", axis=1, tiled=True),
    )
    w_in, w_out, w_up, w_down, w_time, w_class, w_mapup, w_mapdown, w_mod, w_gains = gathered
    feats_low = fourier(my_sigmas, fourier_freqs).astype(jnp.bfloat16)
    onehot_low = (my_classes[:, None] == jnp.arange(NCLASS, dtype=jnp.int32)[None, :]).astype(
        jnp.bfloat16
    )
    gain_values = w_gains.astype(jnp.float32)
    mods, kept_items = map_forward(
        feats_low,
        onehot_low,
        w_time,
        w_class,
        gain_values,
        w_mapup,
        w_mapdown,
        w_mod,
        lambda partial_sum: lax.psum(partial_sum, "mp"),
    )
    slot_count = block_input.shape[0]
    image_ends = jnp.cumsum(my_lengths)
    position = jnp.arange(slot_count, dtype=jnp.int32)
    slot_of = jnp.sum((position[:, None] >= image_ends[None, :]).astype(jnp.int32), axis=1)
    live_rows = (position < image_ends[-1]).astype(jnp.float32)[:, None]
    member = (slot_of[:, None] == jnp.arange(IMG_DEV, dtype=jnp.int32)[None, :]).astype(jnp.float32)
    same_image = slot_of[:, None] == slot_of[None, :]
    attn_mod = 1.0 + jnp.dot(member, mods[:, 0], precision=HIGHEST)
    ff_mod = 1.0 + jnp.dot(member, mods[:, 1], precision=HIGHEST)
    head_scale = headscale_state[0]
    heads_here = head_scale.shape[0]
    width_here = w_in.shape[2]
    head_size = width_here // heads_here
    inputs = block_input.astype(jnp.float32)
    normed_in, in_back = jax.vjp(rms_scale, inputs, attn_mod)
    low_in = normed_in.astype(jnp.bfloat16)
    projected = jnp.einsum("td,dcf->tcf", low_in, w_in, preferred_element_type=jnp.float32)
    queries = projected[:, 0].reshape(slot_count, heads_here, head_size)
    key_rows = projected[:, 1].reshape(slot_count, heads_here, head_size)
    (query_unit, key_unit), cosine_back = jax.vjp(cosine, queries, key_rows, head_scale)
    query_low = query_unit.astype(jnp.bfloat16)
    key_low = key_unit.astype(jnp.bfloat16)
    value_low = projected[:, 2].reshape(slot_count, heads_here, head_size).astype(jnp.bfloat16)
    scores = jnp.einsum("thd,uhd->htu", query_low, key_low, preferred_element_type=jnp.float32)
    scores = jnp.where(same_image[None], scores, MASKED)
    row_max = jnp.max(scores, axis=-1, keepdims=True)
    expon = jnp.exp(scores - row_max)
    row_total = jnp.sum(expon, axis=-1, keepdims=True)
    probabilities = expon / row_total
    log_total = row_max + jnp.log(row_total)
    attended = jnp.einsum(
        "htu,uhd->thd",
        probabilities.astype(jnp.bfloat16),
        value_low,
        preferred_element_type=jnp.float32,
    )
    attended_low = attended.reshape(slot_count, width_here).astype(jnp.bfloat16)
    branch_attn = lax.psum(jnp.dot(attended_low, w_out, preferred_element_type=jnp.float32), "mp")
    middle = inputs + branch_attn
    normed_mid, mid_back = jax.vjp(rms_scale, middle, ff_mod)
    low_mid = normed_mid.astype(jnp.bfloat16)
    hidden = jnp.einsum("td,dcf->tcf", low_mid, w_up, preferred_element_type=jnp.float32)
    gated_vals, gate_back = jax.vjp(geglu_gate, hidden)
    gated_low = gated_vals.astype(jnp.bfloat16)
    branch_ff = lax.psum(
        jnp.dot(gated_low, w_down, preferred_element_type=jnp.float32).astype(jnp.bfloat16), "mp"
    ).astype(jnp.float32)
    layer_out = (live_rows * (middle + branch_ff)).astype(jnp.bfloat16)
    out_grad = live_rows * out_cotangent.astype(jnp.float32)
    grad_branch = out_grad.astype(jnp.bfloat16)
    grad_downproj = jnp.dot(gated_low.T, grad_branch, preferred_element_type=jnp.float32)
    grad_gated = jnp.dot(grad_branch, w_down.T, preferred_element_type=jnp.float32)
    (grad_hidden,) = gate_back(grad_gated)
    grad_hidden_low = grad_hidden.astype(jnp.bfloat16)
    grad_upproj = jnp.einsum(
        "td,tcf->dcf", low_mid, grad_hidden_low, preferred_element_type=jnp.float32
    )
    grad_low_mid = lax.psum(
        jnp.einsum("tcf,dcf->td", grad_hidden_low, w_up, preferred_element_type=jnp.float32), "mp"
    )
    grad_mid_norm, grad_ff_mod = mid_back(grad_low_mid)
    grad_middle = out_grad + grad_mid_norm
    grad_y = grad_middle.astype(jnp.bfloat16)
    grad_outproj = jnp.dot(attended_low.T, grad_y, preferred_element_type=jnp.float32)
    grad_att = (
        jnp.dot(grad_y, w_out.T, preferred_element_type=jnp.float32)
        .astype(jnp.bfloat16)
        .reshape(slot_count, heads_here, head_size)
    )
    again = jnp.einsum("thd,uhd->htu", query_low, key_low, preferred_element_type=jnp.float32)
    again = jnp.where(same_image[None], again, MASKED)
    probs_again = jnp.exp(again - log_total)
    grad_values = jnp.einsum(
        "htu,thd->uhd",
        probs_again.astype(jnp.bfloat16),
        grad_att,
        preferred_element_type=jnp.float32,
    )
    grad_probs = jnp.einsum("thd,uhd->htu", grad_att, value_low, preferred_element_type=jnp.float32)
    inner = jnp.sum(grad_probs * probs_again, axis=-1, keepdims=True)
    grad_scores = (probs_again * (grad_probs - inner)).astype(jnp.bfloat16)
    grad_qunit = jnp.einsum(
        "htu,uhd->thd", grad_scores, key_low, preferred_element_type=jnp.float32
    )
    grad_kunit = jnp.einsum(
        "htu,thd->uhd", grad_scores, query_low, preferred_element_type=jnp.float32
    )
    grad_queries, grad_keys, grad_headscale = cosine_back((grad_qunit, grad_kunit))
    grad_projected = jnp.stack(
        [
            grad_queries.reshape(slot_count, width_here),
            grad_keys.reshape(slot_count, width_here),
            grad_values.reshape(slot_count, width_here),
        ],
        axis=1,
    ).astype(jnp.bfloat16)
    grad_inproj = jnp.einsum(
        "td,tcf->dcf", low_in, grad_projected, preferred_element_type=jnp.float32
    )
    grad_low_in = lax.psum(
        jnp.einsum("tcf,dcf->td", grad_projected, w_in, preferred_element_type=jnp.float32), "mp"
    )
    grad_in_norm, grad_attn_mod = in_back(grad_low_in)
    input_grad = grad_middle + grad_in_norm
    grad_mods = jnp.stack(
        [
            jnp.dot(member.T, grad_attn_mod, precision=HIGHEST),
            jnp.dot(member.T, grad_ff_mod, precision=HIGHEST),
        ],
        axis=1,
    )
    grad_embedded, grad_timeproj, grad_mapup, grad_mapdown, grad_modproj, grad_gains = map_backward(
        kept_items,
        grad_mods,
        feats_low,
        w_mapup,
        w_mapdown,
        w_mod,
        lambda partial_sum: lax.psum(partial_sum, "mp"),
    )
    grad_classemb = jnp.dot(onehot_low.astype(jnp.float32).T, grad_embedded, precision=HIGHEST)
    summed = (
        lax.psum_scatter(grad_inproj, "dp", scatter_dimension=0, tiled=True),
        lax.psum_scatter(grad_outproj, "dp", scatter_dimension=1, tiled=True),
        lax.psum_scatter(grad_upproj, "dp", scatter_dimension=0, tiled=True),
        lax.psum_scatter(grad_downproj, "dp", scatter_dimension=1, tiled=True),
        lax.psum_scatter(grad_timeproj, "dp", scatter_dimension=0, tiled=True),
        lax.psum_scatter(grad_classemb, "dp", scatter_dimension=1, tiled=True),
        lax.psum_scatter(grad_mapup, "dp", scatter_dimension=0, tiled=True),
        lax.psum_scatter(grad_mapdown, "dp", scatter_dimension=1, tiled=True),
        lax.psum_scatter(grad_modproj, "dp", scatter_dimension=0, tiled=True),
        lax.psum_scatter(grad_gains, "dp", scatter_dimension=1, tiled=True),
    )
    shards = list(summed)
    split_squares = jnp.zeros((), jnp.float32)
    for index in (0, 1, 2, 3, 6, 7):
        split_squares = split_squares + jnp.sum(shards[index] * shards[index])
    shared_squares = jnp.zeros((), jnp.float32)
    for index in (4, 5, 8, 9):
        shared_squares = shared_squares + jnp.sum(shards[index] * shards[index])
    squares = split_squares + shared_squares / tensor_count
    head_full = lax.dynamic_update_slice_in_dim(
        jnp.zeros((H,), jnp.float32), grad_headscale, tensor_index * heads_here, 0
    )
    squares_all, head_total = lax.psum((squares, head_full), ("dp", "mp"))
    grad_norm = jnp.sqrt(squares_all + jnp.sum(head_total * head_total))
    factor = CLIP_NORM / jnp.maximum(grad_norm, CLIP_NORM)
    shards.append(lax.dynamic_slice_in_dim(head_total, tensor_index * heads_here, heads_here, 0))
    states = (
        inproj_state,
        outproj_state,
        upproj_state,
        downproj_state,
        timeproj_state,
        classemb_state,
        mapup_state,
        mapdown_state,
        modproj_state,
        gains_state,
        headscale_state,
    )
    rates = learn_rates()
    decays = decay_rates()
    updated = [
        adamw_step(states[index], factor * shards[index], rates[index], decays[index])
        for index in range(11)
    ]
    return (
        layer_out,
        input_grad,
        grad_norm,
        updated[0][0],
        updated[0][1],
        updated[0][2],
        updated[1][0],
        updated[1][1],
        updated[1][2],
        updated[2][0],
        updated[2][1],
        updated[2][2],
        updated[3][0],
        updated[3][1],
        updated[3][2],
        updated[4][0],
        updated[4][1],
        updated[4][2],
        updated[5][0],
        updated[5][1],
        updated[5][2],
        updated[6][0],
        updated[6][1],
        updated[6][2],
        updated[7][0],
        updated[7][1],
        updated[7][2],
        updated[8][0],
        updated[8][1],
        updated[8][2],
        updated[9][0],
        updated[9][1],
        updated[9][2],
        updated[10][0],
        updated[10][1],
        updated[10][2],
    )


def solution(mesh):
    return jax.shard_map(
        per_device,
        mesh=mesh,
        in_specs=(
            P("dp", None),
            P("dp", None),
            P(),
            P(),
            P(),
            P(),
            P(None, "dp", None, "mp"),
            P(None, "mp", "dp"),
            P(None, "dp", None, "mp"),
            P(None, "mp", "dp"),
            P(None, "dp", None),
            P(None, None, "dp"),
            P(None, "dp", None, "mp"),
            P(None, "mp", "dp"),
            P(None, "dp", None, None),
            P(None, None, "dp"),
            P(None, "mp"),
        ),
        out_specs=(
            P("dp", None),
            P("dp", None),
            P(),
            P(None, "dp", None, "mp"),
            P("dp", None, "mp"),
            P("dp", None, "mp"),
            P(None, "mp", "dp"),
            P("mp", "dp"),
            P("mp", "dp"),
            P(None, "dp", None, "mp"),
            P("dp", None, "mp"),
            P("dp", None, "mp"),
            P(None, "mp", "dp"),
            P("mp", "dp"),
            P("mp", "dp"),
            P(None, "dp", None),
            P("dp", None),
            P("dp", None),
            P(None, None, "dp"),
            P(None, "dp"),
            P(None, "dp"),
            P(None, "dp", None, "mp"),
            P("dp", None, "mp"),
            P("dp", None, "mp"),
            P(None, "mp", "dp"),
            P("mp", "dp"),
            P("mp", "dp"),
            P(None, "dp", None, None),
            P("dp", None, None),
            P("dp", None, None),
            P(None, None, "dp"),
            P(None, "dp"),
            P(None, "dp"),
            P(None, "mp"),
            P("mp"),
            P("mp"),
        ),
        check_vma=False,
    )
```

profile of v0, /device:TPU:0, one launch (start us, length us, event | category | flops | bytes accessed | tf_op | source)
XLA Modules:
  0.0 1781.8 jit_solution(663361408794224039)
XLA Ops:
  24.9 22.3 %all-gather.9 = bf16[8,96,3]{1,2,0:T(4,128)(2,1)S(1)} all-gather(bf16[1,96,3]{1,2,0:T(4,128)(2,1)S(1)} %bitcast.544), channel_id=1, replica_groups=mesh['dp'=8,'mp'=4] {'dp'}, dimensions={0}, use_global_device_ids=true | all-gather | bytes 5184 | tf_op jit(solution)/shard_map/all_gather | solution.py:160
  49.2 29.3 %all-gather.6 = bf16[1,256,1024]{2,1,0:T(8,128)(2,1)} all-gather(bf16[1,256,128]{2,1,0:T(8,128)(2,1)S(1)} %slice.340), channel_id=8, replica_groups=mesh['dp'=8,'mp'=4] {'dp'}, dimensions={2}, use_global_device_ids=true | all-gather | bytes 589824 | tf_op jit(solution)/shard_map/all_gather | solution.py:152
  78.5 34.9 %all-gather.3 = bf16[1,576,768]{1,2,0:T(8,128)(2,1)S(1)} all-gather(bf16[1,576,96]{1,2,0:T(8,128)(2,1)S(1)} %slice.339), channel_id=5, replica_groups=mesh['dp'=8,'mp'=4] {'dp'}, dimensions={2}, use_global_device_ids=true | all-gather | bytes 995328 | tf_op jit(solution)/shard_map/all_gather | solution.py:158
  123.7 39.4 %all-gather.22.cloned.1.call-done = bf16[1,768,2,576]{3,2,0,1:T(2,128)(2,1)} async-done(((bf16[1,96,2,576]{3,2,0,1:T(2,128)(2,1)}), bf16[1,768,2,576]{3,2,0,1:T(2,128)(2,1)}) %all-gather.22.cloned.1.call-update) | async-done | bytes 1769488 | tf_op jit(solution)/shard_map/all_gather | solution.py:157
  173.4 11.6 psum.56
  185.1 40.1 %all-gather.24.cloned.1.call-done = bf16[1,768,2,1024]{3,1,2,0:T(8,128)(2,1)} async-done(((bf16[1,96,2,1024]{3,1,2,0:T(8,128)(2,1)}), bf16[1,768,2,1024]{3,1,2,0:T(8,128)(2,1)}) %all-gather.24.cloned.1.call-update) | async-done | bytes 3145744 | tf_op jit(solution)/shard_map/all_gather | solution.py:159
  233.9 37.7 %all-gather.26.cloned.1.call-done = bf16[1,1024,3,256]{1,3,2,0:T(8,128)(2,1)} async-done(((bf16[1,128,3,256]{1,3,2,0:T(8,128)(2,1)}), bf16[1,1024,3,256]{1,3,2,0:T(8,128)(2,1)}) %all-gather.26.cloned.1.call-update) | async-done | bytes 1572880 | tf_op jit(solution)/shard_map/all_gather | solution.py:151
  285.1 9.1 fusion
  294.2 8.5 fusion.72
  327.1 77.1 %all-reduce.12.cloned.1.call-done = f32[1024,1024]{0,1:T(8,128)} async-done(((f32[1024,1024]{0,1:T(8,128)}), f32[1024,1024]{0,1:T(8,128)}) %all-reduce.12.cloned.1.call-update) | async-done | bytes 4194320 | tf_op jit(solution)/shard_map/psum | solution.py:216
  410.7 57.2 %all-gather.28.cloned.1.call-done = bf16[1,1024,2,768]{3,1,2,0:T(8,128)(2,1)} async-done(((bf16[1,128,2,768]{3,1,2,0:T(8,128)(2,1)}), bf16[1,1024,2,768]{3,1,2,0:T(8,128)(2,1)}) %all-gather.28.cloned.1.call-update) | async-done | bytes 3145744 | tf_op jit(solution)/shard_map/all_gather | solution.py:153
  473.5 7.5 fusion.26
  496.1 78.9 %all-reduce.16.cloned.1.call-done = f32[1024,1024]{0,1:T(8,128)} async-done(((f32[1024,1024]{0,1:T(8,128)}), f32[1024,1024]{0,1:T(8,128)}) %all-reduce.16.cloned.1.call-update) | async-done | bytes 4194320 | tf_op jit(solution)/shard_map/psum | solution.py:236
  580.6 48.1 %all-reduce.14.cloned.1.call-done = bf16[1024,1024]{0,1:T(8,128)(2,1)} async-done(((bf16[1024,1024]{0,1:T(8,128)(2,1)}), bf16[1024,1024]{0,1:T(8,128)(2,1)}) %all-reduce.14.cloned.1.call-update) | async-done | bytes 2097168 | tf_op jit(solution)/shard_map/psum | solution.py:223
  628.7 7.5 fusion.11
  638.9 8.8 fusion.69
  647.8 15.3 multiply_reduce_fusion
  663.1 10.9 multiply_convert_fusion
  674.1 7.5 multiply_reduce_fusion.4
  707.8 73.8 %all-reduce.18.cloned.1.call-done = f32[1024,1024]{0,1:T(8,128)} async-done(((f32[1024,1024]{0,1:T(8,128)}), f32[1024,1024]{0,1:T(8,128)}) %all-reduce.18.cloned.1.call-update) | async-done | bytes 4194320 | tf_op jit(solution)/shard_map/psum | solution.py:278
  790.8 10.1 psum.61
  830.0 9.5 fusion.124
  865.8 48.3 %reduce-scatter.28.cloned.1.call-done = f32[96,3]{1,0:T(8,128)} async-done(((f32[768,3]{1,0:T(8,128)}), f32[96,3]{1,0:T(8,128)}) %reduce-scatter.28.cloned.1.call-update) | async-done | bytes 1168
  915.6 76.5 %reduce-scatter.18.cloned.1.call-done = f32[768,128]{1,0:T(8,128)} async-done(((f32[768,1024]{1,0:T(8,128)}), f32[768,128]{1,0:T(8,128)}) %reduce-scatter.18.cloned.1.call-update) | async-done | bytes 393232 | tf_op jit(solution)/shard_map/reduce_scatter | solution.py:304
  993.7 151.3 %all-reduce.20.cloned.1.call-done = f32[768,2,576]{2,1,0:T(2,128)} async-done(((f32[768,2,576]{2,1,0:T(2,128)}), f32[768,2,576]{2,1,0:T(2,128)}) %all-reduce.20.cloned.1.call-update) | async-done | bytes 3538960
  1147.1 67.5 %reduce-scatter.20.cloned.1.call-done = f32[576,96]{0,1:T(8,128)} async-done(((f32[576,768]{0,1:T(8,128)}), f32[576,96]{0,1:T(8,128)}) %reduce-scatter.20.cloned.1.call-update) | async-done | bytes 221200 | tf_op jit(solution)/shard_map/reduce_scatter | solution.py:308
  1216.2 76.0 %reduce-scatter.12.cloned.1.call-done = f32[128,3,256]{0,2,1:T(8,128)} async-done(((f32[1024,3,256]{0,2,1:T(8,128)}), f32[128,3,256]{0,2,1:T(8,128)}) %reduce-scatter.12.cloned.1.call-update) | async-done | bytes 393232 | tf_op jit(solution)/shard_map/reduce_scatter | solution.py:301
  1295.2 68.8 %reduce-scatter.22.cloned.1.call-done = f32[96,768]{1,0:T(8,128)} async-done(((f32[768,768]{1,0:T(8,128)}), f32[96,768]{1,0:T(8,128)}) %reduce-scatter.22.cloned.1.call-update) | async-done | bytes 294928 | tf_op jit(solution)/shard_map/reduce_scatter | solution.py:305
  1365.6 75.5 %reduce-scatter.24.cloned.1.call-done = f32[1000,96]{0,1:T(8,128)} async-done(((f32[1000,768]{0,1:T(8,128)}), f32[1000,96]{0,1:T(8,128)}) %reduce-scatter.24.cloned.1.call-update) | async-done | bytes 384016 | tf_op jit(solution)/shard_map/reduce_scatter | solution.py:306
  1444.1 117.5 %reduce-scatter.16.cloned.1.call-done = f32[128,2,768]{2,0,1:T(8,128)} async-done(((f32[1024,2,768]{2,0,1:T(8,128)}), f32[128,2,768]{2,0,1:T(8,128)}) %reduce-scatter.16.cloned.1.call-update) | async-done | bytes 786448 | tf_op jit(solution)/shard_map/reduce_scatter | solution.py:303
  1566.1 116.2 %reduce-scatter.26.cloned.1.call-done = f32[96,2,1024]{2,0,1:T(8,128)} async-done(((f32[768,2,1024]{2,0,1:T(8,128)}), f32[96,2,1024]{2,0,1:T(8,128)}) %reduce-scatter.26.cloned.1.call-update) | async-done | bytes 786448 | tf_op jit(solution)/shard_map/reduce_scatter | solution.py:309
  1691.1 39.6 %all-reduce.5 = (f32[]{:T(128)}, f32[16]{0:T(128)S(1)}) all-reduce(f32[]{:T(128)S(6)} %add.376, f32[16]{0:T(128)S(1)} %dynamic_update_slice.3), channel_id=1, replica_groups=mesh['dp'=8,'mp'=4] {'dp','mp'}, use_global_device_ids=true, to_apply=%region_48.49 | all-reduce | flops 17 | bytes 136 | tf_op jit(solution)/shard_map/psum | solution.py:323
  (474 shorter events, 273.9 us)
Async XLA Ops:
  7.2 111.4 %all-gather.18.cloned.1.call-start = ((), (), s32[]{:S(2)}) async-start(), calls=%async_computation.21 | async-start | bytes 1327104 | tf_op jit(solution)/shard_map/all_gather | solution.py:155
  8.9 111.8 %all-gather.20.cloned.1.call-start = ((), (), s32[]{:S(2)}) async-start(), calls=%async_computation.22 | async-start | bytes 1769472 | tf_op jit(solution)/shard_map/all_gather | solution.py:156
  10.7 152.3 %all-gather.22.cloned.1.call-start = ((), (), s32[]{:S(2)}) async-start(), calls=%async_computation.23 | async-start | bytes 2211840 | tf_op jit(solution)/shard_map/all_gather | solution.py:157
  12.7 212.5 %all-gather.24.cloned.1.call-start = ((), (), s32[]{:S(2)}) async-start(), calls=%async_computation.24 | async-start | bytes 3538944 | tf_op jit(solution)/shard_map/all_gather | solution.py:159
  18.6 253.0 %all-gather.26.cloned.1.call-start = ((), (), s32[]{:S(2)}) async-start(), calls=%async_computation.25 | async-start | bytes 1769472 | tf_op jit(solution)/shard_map/all_gather | solution.py:151
  19.9 93.6 %copy-start.25 = (f32[1,128,3,256]{1,3,2,0:T(8,128)}, f32[1,128,3,256]{1,3,2,0:T(8,128)S(1)}, u32[]{:S(2)}) copy-start(f32[1,128,3,256]{1,3,2,0:T(8,128)S(1)} %copy.328) | copy-start | bytes 1179652
  20.7 297.0 %all-gather.30.cloned.1.call-start = ((), (), s32[]{:S(2)}) async-start(), calls=%async_computation.27 | async-start | bytes 1769472 | tf_op jit(solution)/shard_map/all_gather | solution.py:154
  22.4 381.8 %all-reduce.12.cloned.1.call-start = ((), (), s32[]{:S(2)}) async-start(), calls=%async_computation.9 | async-start | bytes 8388608 | tf_op jit(solution)/shard_map/psum | solution.py:216
  23.3 97.5 %copy-start.116 = (s32[4]{0:T(128)}, s32[4]{0:T(128)S(1)}, u32[]{:S(2)}) copy-start(s32[4]{0:T(128)S(1)} %dynamic_slice.14) | copy-start | bytes 52
  47.3 122.4 %copy-start.87 = (f32[768]{0:T(1024)}, f32[768]{0:T(1024)S(1)}, u32[]{:S(2)}) copy-start(f32[768]{0:T(1024)S(1)} %get-tuple-element.225) | copy-start | bytes 9220
  47.3 177.9 %copy-start.85 = (f32[768]{0:T(1024)}, f32[768]{0:T(1024)S(1)}, u32[]{:S(2)}) copy-start(f32[768]{0:T(1024)S(1)} %get-tuple-element.224) | copy-start | bytes 9220
  117.9 286.3 %copy-start.3 = (bf16[1024,1024]{0,1:T(8,128)(2,1)}, bf16[1024,1024]{0,1:T(8,128)(2,1)S(1)}, u32[]{:S(2)}) copy-start(bf16[1024,1024]{0,1:T(8,128)(2,1)S(1)} %copy.258) | copy-start | bytes 6291460
  118.4 111.1 %copy-start.91 = (f32[1024]{0:T(1024)}, f32[1024]{0:T(1024)S(1)}, u32[]{:S(2)}) copy-start(f32[1024]{0:T(1024)S(1)} %fusion.172) | copy-start | bytes 12292
  306.3 161.6 %all-gather.28.cloned.1.call-start = ((), (), s32[]{:S(2)}) async-start(), calls=%async_computation.26 | async-start | bytes 3538944 | tf_op jit(solution)/shard_map/all_gather | solution.py:153
  312.0 263.0 %all-reduce.16.cloned.1.call-start = ((), (), s32[]{:S(2)}) async-start(), calls=%async_computation.11 | async-start | bytes 8388608 | tf_op jit(solution)/shard_map/psum | solution.py:236
  317.6 311.1 %copy-start.102 = (f32[1024]{0:T(1024)}, f32[1024]{0:T(1024)S(1)}, u32[]{:S(2)}) copy-start(f32[1024]{0:T(1024)S(1)} %fusion.171) | copy-start | bytes 12292
  490.7 138.0 %all-reduce.14.cloned.1.call-start = ((), (), s32[]{:S(2)}) async-start(), calls=%async_computation.10 | async-start | bytes 4194304 | tf_op jit(solution)/shard_map/psum | solution.py:223
  495.4 286.2 %all-reduce.18.cloned.1.call-start = ((), (), s32[]{:S(2)}) async-start(), calls=%async_computation.12 | async-start | bytes 8388608 | tf_op jit(solution)/shard_map/psum | solution.py:278
  496.1 132.6 %copy-start.20 = (bf16[1024,1024]{0,1:T(8,128)(2,1)S(1)}, bf16[1024,1024]{0,1:T(8,128)(2,1)}, u32[]{:S(2)}) copy-start(bf16[1024,1024]{0,1:T(8,128)(2,1)} %copy.271) | copy-start | bytes 6291460
  695.8 156.9 %reduce-scatter.14.cloned.1.call-start = ((), (), s32[]{:S(2)}) async-start(), calls=%async_computation.14 | async-start | bytes 1179648 | tf_op jit(solution)/shard_map/reduce_scatter | solution.py:302
  700.8 80.8 %copy-start.4 = (bf16[1024,1024]{0,1:T(8,128)(2,1)S(1)}, bf16[1024,1024]{0,1:T(8,128)(2,1)}, u32[]{:S(2)}) copy-start(bf16[1024,1024]{0,1:T(8,128)(2,1)} %copy-done.3) | copy-start | bytes 6291460
  700.8 80.8 %copy-start.92 = (f32[1024]{0:T(1024)S(1)}, f32[1024]{0:T(1024)}, u32[]{:S(2)}) copy-start(f32[1024]{0:T(1024)} %copy-done.91) | copy-start | bytes 12292
  700.8 213.2 %reduce-scatter.28.cloned.1.call-start = ((), (), s32[]{:S(2)}) async-start(), calls=%async_computation.28 | async-start | bytes 442368
  707.8 78.7 %copy-start.109 = (f32[4]{0:T(128)S(1)}, f32[4]{0:T(128)}, u32[]{:S(2)}) copy-start(f32[4]{0:T(128)} %copy-done.108) | copy-start | bytes 52
  802.4 189.6 %reduce-scatter.18.cloned.1.call-start = ((), (), s32[]{:S(2)}) async-start(), calls=%async_computation.16 | async-start | bytes 3538944 | tf_op jit(solution)/shard_map/reduce_scatter | solution.py:304
  808.0 337.0 %all-reduce.20.cloned.1.call-start = ((), (), s32[]{:S(2)}) async-start(), calls=%async_computation.29 | async-start | bytes 7864320
  815.0 399.6 %reduce-scatter.20.cloned.1.call-start = ((), (), s32[]{:S(2)}) async-start(), calls=%async_computation.17 | async-start | bytes 2211840 | tf_op jit(solution)/shard_map/reduce_scatter | solution.py:308
  818.0 474.2 %reduce-scatter.12.cloned.1.call-start = ((), (), s32[]{:S(2)}) async-start(), calls=%async_computation.13 | async-start | bytes 3538944 | tf_op jit(solution)/shard_map/reduce_scatter | solution.py:301
  823.3 540.7 %reduce-scatter.22.cloned.1.call-start = ((), (), s32[]{:S(2)}) async-start(), calls=%async_computation.18 | async-start | bytes 2654208 | tf_op jit(solution)/shard_map/reduce_scatter | solution.py:305
  826.5 614.6 %reduce-scatter.24.cloned.1.call-start = ((), (), s32[]{:S(2)}) async-start(), calls=%async_computation.19 | async-start | bytes 3538944 | tf_op jit(solution)/shard_map/reduce_scatter | solution.py:306
  829.8 731.8 %reduce-scatter.16.cloned.1.call-start = ((), (), s32[]{:S(2)}) async-start(), calls=%async_computation.15 | async-start | bytes 7077888 | tf_op jit(solution)/shard_map/reduce_scatter | solution.py:303
  839.6 842.8 %reduce-scatter.26.cloned.1.call-start = ((), (), s32[]{:S(2)}) async-start(), calls=%async_computation.20 | async-start | bytes 7077888 | tf_op jit(solution)/shard_map/reduce_scatter | solution.py:309
  (124 other events, 1715.6 us)
Sparse Core Ops, SparseCore 0:
  10.8 43.7 all-gather.17
  57.4 54.9 all-gather.19
  115.2 47.8 all-gather.21
  165.6 59.5 all-gather.23
  227.7 43.9 all-gather.25
  274.1 43.4 all-gather.29
  320.5 83.7 all-reduce.11
  407.3 60.6 all-gather.27
  490.8 84.0 all-reduce.15
  577.1 51.5 all-reduce.13
  696.0 85.5 all-reduce.17
  785.4 64.1 reduce-scatter.13
  853.7 60.2 reduce-scatter.27
  918.0 74.0 reduce-scatter.17
  996.5 148.4 all-reduce.19
  1148.7 65.8 reduce-scatter.19
  1218.1 74.0 reduce-scatter.11
  1295.5 68.3 reduce-scatter.21
  1367.5 73.5 reduce-scatter.23
  1444.5 117.0 reduce-scatter.15
  1565.2 117.0 reduce-scatter.25
where the time goes:
time: 1790 us; the launch traced here: 1780 us
  waiting for transfers between devices  1250 us (70%)
  matrix products  154 us (9%)
  blocking collectives  148 us (8%)
  other arithmetic  110 us (6%)
  local copies, waits for them, and re-layouts  93 us (5%)
  between operations  26 us (1%)
    unnamed x23, waiting for transfers between devices  200 us
    reduce_scatter x1, waiting for transfers between devices, per_device(): lax.psum_scatter(grad_upproj, 'dp', scatter_dimension=0, tiled=True)  118 us
    reduce_scatter x1, waiting for transfers between devices, per_device(): lax.psum_scatter(grad_modproj, 'dp', scatter_dimension=0, tiled=True)  116 us
    psum x1, waiting for transfers between devices, per_device(): lax.psum(jnp.einsum('tcf,dcf->td', grad_hidden_low, w_up, preferred_eleme...  78.9 us
    psum x1, waiting for transfers between devices, per_device(): lax.psum(jnp.dot(attended_low, w_out, preferred_element_type=jnp.float32)...  77.1 us
    reduce_scatter x1, waiting for transfers between devices, per_device(): lax.psum_scatter(grad_downproj, 'dp', scatter_dimension=1, tiled=True)  76.5 us
    reduce_scatter x1, waiting for transfers between devices, per_device(): lax.psum_scatter(grad_inproj, 'dp', scatter_dimension=0, tiled=True)  76 us
    reduce_scatter x1, waiting for transfers between devices, per_device(): lax.psum_scatter(grad_classemb, 'dp', scatter_dimension=1, tiled=True)  75.5 us
  transfers between devices with their start and end apart: 21, of which 17 were waited for; matrix products, arithmetic and copies ran while one was open for 11% of the time, Pallas kernels for 0%

commit v1 on v0

v1 whole, which is shorter than its diff:
```python
import functools
import math

import jax
import jax.numpy as jnp
from jax import lax
from jax.experimental import pallas as pl
from jax.experimental.pallas import tpu as pltpu
from jax.sharding import PartitionSpec as P

D = 1024
H = 16
FF = 3072
DM = 768
MFF = 2304
NCLASS = 1000
IMG_DEV = 4
STEP = 10

EPSILON = 1e-06
BETA_ONE = 0.9
BETA_TWO = 0.95
ADAM_EPSILON = 1e-08
CLIP_NORM = 1.0
MASKED = -1e30
MESH = pl.DeviceIdType.MESH
VMEM_BYTES = 60 * 2**20
F32 = jnp.float32
BF16 = jnp.bfloat16


def minor_size(count):
    return 1 << ((count.bit_length() - 1) // 2)


def fourier(sigmas, fourier_freqs):
    angles = 2.0 * math.pi * (jnp.log(sigmas) / 4.0)[:, None] * fourier_freqs[None, :]
    return jnp.concatenate([jnp.cos(angles), jnp.sin(angles)], axis=1)


def learn_rates():
    return (
        2.5 * D ** (-0.5),
        2.5 * (D // 64) ** (-0.5),
        2.5 * D ** (-0.5),
        2.5 * FF ** (-0.5),
        2.5 * DM ** (-0.5),
        2.5,
        2.5 * DM ** (-0.5),
        2.5 * MFF ** (-0.5),
        1.25 * DM ** (-0.5),
        0.25,
        7.5,
    )


def decay_rates():
    return (0.01, 0.01, 0.01, 0.01, 0.01, 0.01, 0.01, 0.01, 0.01, 0.0, 0.0)


def adamw_step(state, gradient, rate, decay):
    keep_rate = 1.0 - (1.0 + STEP) ** (-0.75)
    first = BETA_ONE * state[1] + (1.0 - BETA_ONE) * gradient
    second = BETA_TWO * state[2] + (1.0 - BETA_TWO) * gradient * gradient
    first_hat = first / (1.0 - BETA_ONE**STEP)
    second_hat = second / (1.0 - BETA_TWO**STEP)
    weight = state[0] * (1.0 - rate * decay) - rate * first_hat / (
        jnp.sqrt(second_hat) + ADAM_EPSILON
    )
    average = keep_rate * state[3] + (1.0 - keep_rate) * weight
    return (jnp.stack([weight, average]), first, second)


def dot_nn(a, b):
    return lax.dot_general(a, b, (((1,), (0,)), ((), ())), preferred_element_type=F32)


def dot_nt(a, b):
    return lax.dot_general(a, b, (((1,), (1,)), ((), ())), preferred_element_type=F32)


def dot_tn(a, b):
    return lax.dot_general(a, b, (((0,), (0,)), ((), ())), preferred_element_type=F32)


def two_part(dot, exact, wide):
    high = wide.astype(BF16)
    low = (wide - high.astype(F32)).astype(BF16)
    return dot(exact, high) + dot(exact, low)


def two_part_left(dot, wide, exact):
    high = wide.astype(BF16)
    low = (wide - high.astype(F32)).astype(BF16)
    return dot(high, exact) + dot(low, exact)


def gelu_parts(b):
    cdf = 0.5 * (1.0 + lax.erf(b * (1.0 / math.sqrt(2.0))))
    pdf = jnp.exp(-0.5 * b * b) * (1.0 / math.sqrt(2.0 * math.pi))
    return b * cdf, cdf + b * pdf


def greet(peers):
    barrier = pltpu.get_barrier_semaphore()
    total = 0
    for count, peer_of in peers:

        def say(k, carry, peer_of=peer_of):
            pl.semaphore_signal(barrier, inc=1, device_id=peer_of(k), device_id_type=MESH)
            return carry

        lax.fori_loop(1, count, say, 0)
        total += count - 1
    pl.semaphore_wait(barrier, total)


class Exchange:
    def __init__(self, count, me, device_of, send_sem, recv_sem):
        self.count, self.me, self.device_of = count, me, device_of
        self.send_sem, self.recv_sem = send_sem, recv_sem

    def _copy(self, k, src_of, dst, slot):
        peer = lax.rem(self.me + k, self.count)
        return pltpu.make_async_remote_copy(
            src_ref=src_of(peer),
            dst_ref=dst.at[slot],
            send_sem=self.send_sem.at[k],
            recv_sem=self.recv_sem.at[k],
            device_id=self.device_of(peer),
            device_id_type=MESH,
        )

    def start(self, src_of, dst):
        def body(k, carry):
            self._copy(k, src_of, dst, self.me).start()
            return carry

        lax.fori_loop(1, self.count, body, 0)

    def wait(self, src_of, dst):
        def body(k, carry):
            self._copy(k, src_of, dst, lax.rem(self.me + self.count - k, self.count)).wait()
            return carry

        lax.fori_loop(1, self.count, body, 0)

    def run(self, src_of, dst):
        self.start(src_of, dst)
        self.wait(src_of, dst)


def total_of(ref, count):
    value = ref[0]
    for index in range(1, count):
        value = value + ref[index]
    return value


def mean_square(blocks):
    sums = jnp.sum(jnp.sum(blocks, axis=0), axis=-1, keepdims=True)
    return sums * (1.0 / DM)


def rms_blocks(blocks):
    factor = lax.rsqrt(mean_square(blocks * blocks) + EPSILON)
    return factor


def rms_blocks_back(blocks, factor, gain_grad):
    inner = mean_square(blocks * gain_grad)
    return factor[None] * gain_grad - blocks * (factor * factor * factor * inner)[None]


def front_kernel(
    n_dp, n_mp,
    shard_ref, feats_ref, wt_ref, ecols_ref, gains_ref, wmu_ref, wmd_ref, wmod_ref,
    wg_ref, mods_ref, emb_ref, hid_ref, gated_ref, mixed_ref,
    send_a, recv_a, own_a, send_h, recv_h, own_g, recv_g, own_x, recv_x, own_m, send_o, recv_o,
    dp_ss, dp_rs, mp_ss, mp_rs, z_ss, z_rs, y_ss, y_rs,
):
    d, m = lax.axis_index("dp"), lax.axis_index("mp")
    n_y = minor_size(n_dp)
    n_z = n_dp // n_y
    z, y = lax.div(d, n_y), lax.rem(d, n_y)
    images = feats_ref.shape[0]
    rows = shard_ref.shape[1]
    greet(
        [
            (n_dp, lambda k: (lax.rem(d + k, n_dp), m)),
            (n_mp, lambda k: (d, lax.rem(m + k, n_mp))),
        ]
    )

    def block(dd):
        return wg_ref.at[:, pl.ds(pl.multiple_of(dd * rows, rows), rows), :]

    wg_ref[:, pl.ds(pl.multiple_of(d * rows, rows), rows), :] = shard_ref[...]

    def z_copy(kz, from_z):
        to = lax.rem(z + kz, n_z) * n_y + y
        return pltpu.make_async_remote_copy(
            src_ref=block(d), dst_ref=block(from_z * n_y + y), send_sem=z_ss.at[kz],
            recv_sem=z_rs.at[kz], device_id=(to, m), device_id_type=MESH)

    def y_copy(kz, ky, out_block, in_block):
        to = z * n_y + lax.rem(y + ky, n_y)
        return pltpu.make_async_remote_copy(
            src_ref=block(out_block), dst_ref=block(in_block), send_sem=y_ss.at[kz, ky],
            recv_sem=y_rs.at[kz, ky], device_id=(to, m), device_id_type=MESH)

    def z_start(kz, carry):
        z_copy(kz, z).start()
        return carry

    def y_start(kz):
        mine = lax.rem(z + n_z - kz, n_z) * n_y + y

        def body(ky, carry):
            y_copy(kz, ky, mine, mine).start()
            return carry

        lax.fori_loop(1, n_y, body, 0)

    def forward(kz):
        z_copy(kz, lax.rem(z + n_z - kz, n_z)).wait_recv()
        y_start(kz)

    def finish(kz, carry):
        z_from = lax.rem(z + n_z - kz, n_z)

        def body(ky, inner):
            y_copy(kz, ky, z_from * n_y + y, z_from * n_y + lax.rem(y + n_y - ky, n_y)).wait()
            return inner

        lax.fori_loop(1, n_y, body, 0)
        return carry

    lax.fori_loop(1, n_z, z_start, 0)
    y_start(0)

    def dp_ex(stage):
        return Exchange(n_dp, d, lambda p: (p, m), dp_ss.at[stage], dp_rs.at[stage])

    feats = feats_ref[...]
    for p in range(n_dp):
        send_a[p] = dot_nn(feats, wt_ref[p])
    ex = dp_ex(0)
    ex.start(lambda p: send_a.at[p], recv_a)
    recv_a[d] = send_a[d]
    ex.wait(lambda p: send_a.at[p], recv_a)
    own_a[0:images, :] = total_of(recv_a, n_dp) + ecols_ref[...]
    own_a[images:, :] = gains_ref[...]
    ex = dp_ex(1)
    ex.start(lambda p: own_a, emb_ref)
    emb_ref[d] = own_a[...]
    ex.wait(lambda p: own_a, emb_ref)
    gains = emb_ref[:, images:, :]
    emb = emb_ref[:, 0:images, :]
    unit = emb * rms_blocks(emb)[None] * gains[:, 0:1, :]
    unit_factor = rms_blocks(unit)
    own_x[0] = (emb_ref[d][0:images] * rms_blocks(emb)) * emb_ref[d][images : images + 1]
    unit_own = own_x[0]
    pre_own = (unit_own * unit_factor * emb_ref[d][images + 1 : images + 2]).astype(BF16)
    for c in range(2):
        part = dot_nn(pre_own, wmu_ref[c])
        for p in range(n_dp):
            send_h[p, c] = part[p * IMG_DEV : (p + 1) * IMG_DEV, :]
    ex = dp_ex(2)
    ex.start(lambda p: send_h.at[p], recv_h)
    recv_h[d] = send_h[d]
    ex.wait(lambda p: send_h.at[p], recv_h)
    hidden = total_of(recv_h, n_dp)
    hid_ref[...] = hidden
    own_g[...] = (hidden[0] * gelu_parts(hidden[1])[0]).astype(BF16).astype(F32)
    ex = dp_ex(3)
    ex.start(lambda p: own_g, recv_g)
    recv_g[d] = own_g[...]
    ex.wait(lambda p: own_g, recv_g)
    for p in range(n_dp):
        gated_ref[p * IMG_DEV : (p + 1) * IMG_DEV, :] = recv_g[p]
    own_x[0] = dot_nt(gated_ref[...].astype(BF16), wmd_ref[...])
    ex = Exchange(n_mp, m, lambda p: (d, p), mp_ss.at[0], mp_rs.at[0])
    ex.start(lambda p: own_x.at[0], recv_x)
    recv_x[m] = own_x[0]
    ex.wait(lambda p: own_x.at[0], recv_x)
    own_m[...] = total_of(recv_x, n_mp) + unit_own
    ex = dp_ex(4)
    ex.start(lambda p: own_m, mixed_ref)
    mixed_ref[d] = own_m[...]
    ex.wait(lambda p: own_m, mixed_ref)
    mixed_factor = rms_blocks(mixed_ref[...])
    cond_own = (own_m[...] * mixed_factor * emb_ref[d][images + 2 : images + 3]).astype(BF16)
    for c in range(2):
        part = dot_nn(cond_own, wmod_ref[c])
        for p in range(n_dp):
            send_o[p, c] = part[p * IMG_DEV : (p + 1) * IMG_DEV, :]
    ex = dp_ex(5)
    ex.start(lambda p: send_o.at[p], recv_o)
    for kz in range(1, n_z):
        forward(kz)
    recv_o[d] = send_o[d]
    ex.wait(lambda p: send_o.at[p], recv_o)
    mods_ref[...] = total_of(recv_o, n_dp)

    def z_done(kz, carry):
        z_copy(kz, z).wait_send()
        return carry

    lax.fori_loop(0, n_z, finish, 0)
    lax.fori_loop(1, n_z, z_done, 0)


def vmem_specs(count):
    return [pl.BlockSpec(memory_space=pltpu.VMEM)] * count


def front(n_dp, n_mp, shard, feats_own, w_time, e_cols, gains_own, w_mapup, w_mapdown, w_mod):
    images, part = feats_own.shape
    units = w_mapup.shape[2]
    n_y = minor_size(n_dp)
    n_z = n_dp // n_y
    shape = lambda *dims: jax.ShapeDtypeStruct(dims, F32)
    return pl.pallas_call(
        functools.partial(front_kernel, n_dp, n_mp),
        out_shape=(
            jax.ShapeDtypeStruct((shard.shape[0], shard.shape[1] * n_dp, shard.shape[2]), BF16),
            shape(2, IMG_DEV, D),
            shape(n_dp, images + 8, part),
            shape(2, IMG_DEV, units),
            shape(images, units),
            shape(n_dp, images, part),
        ),
        in_specs=vmem_specs(8),
        out_specs=tuple(vmem_specs(6)),
        scratch_shapes=[
            pltpu.VMEM((n_dp, images, part), F32),
            pltpu.VMEM((n_dp, images, part), F32),
            pltpu.VMEM((images + 8, part), F32),
            pltpu.VMEM((n_dp, 2, IMG_DEV, units), F32),
            pltpu.VMEM((n_dp, 2, IMG_DEV, units), F32),
            pltpu.VMEM((IMG_DEV, units), F32),
            pltpu.VMEM((n_dp, IMG_DEV, units), F32),
            pltpu.VMEM((1, images, part), F32),
            pltpu.VMEM((n_mp, images, part), F32),
            pltpu.VMEM((images, part), F32),
            pltpu.VMEM((n_dp, 2, IMG_DEV, D), F32),
            pltpu.VMEM((n_dp, 2, IMG_DEV, D), F32),
            pltpu.SemaphoreType.DMA((6, n_dp)),
            pltpu.SemaphoreType.DMA((6, n_dp)),
            pltpu.SemaphoreType.DMA((1, n_mp)),
            pltpu.SemaphoreType.DMA((1, n_mp)),
            pltpu.SemaphoreType.DMA((n_z,)),
            pltpu.SemaphoreType.DMA((n_z,)),
            pltpu.SemaphoreType.DMA((n_z, n_y)),
            pltpu.SemaphoreType.DMA((n_z, n_y)),
        ],
        compiler_params=pltpu.CompilerParams(
            collective_id=0, has_side_effects=True, vmem_limit_bytes=VMEM_BYTES
        ),
        name="front",
    )(shard, feats_own, w_time, e_cols, gains_own, w_mapup, w_mapdown, w_mod)


def back_kernel(
    n_dp, n_mp,
    grads_ref, dmods_ref, feats_ref, onehot_ref, wmu_ref, wmd_ref, wmod_ref,
    emb_ref, hid_ref, gated_ref, mixed_ref,
    gshard_ref, gmod_ref, gmd_ref, gmu_ref, gtime_ref, gclass_ref, ggain_ref,
    recv_q, own_q, recv_d, full_d, own_c, recv_c, send_g, recv_g, own_h, recv_h, full_h,
    own_p, recv_p, own_s, recv_s,
    recv_y, send_z, recv_z,
    dp_ss, dp_rs, mp_ss, mp_rs, z_ss, z_rs, y_ss, y_rs,
):
    d, m = lax.axis_index("dp"), lax.axis_index("mp")
    n_y = minor_size(n_dp)
    n_z = n_dp // n_y
    z, y = lax.div(d, n_y), lax.rem(d, n_y)
    images = feats_ref.shape[0]
    rows = gshard_ref.shape[1]
    greet(
        [
            (n_dp, lambda k: (lax.rem(d + k, n_dp), m)),
            (n_mp, lambda k: (d, lax.rem(m + k, n_mp))),
        ]
    )

    def piece(dd):
        return grads_ref.at[:, pl.ds(pl.multiple_of(dd * rows, rows), rows), :]

    def y_copy(kz, ky):
        to_y = lax.rem(y + ky, n_y)
        return pltpu.make_async_remote_copy(
            src_ref=piece(lax.rem(z + kz, n_z) * n_y + to_y), dst_ref=recv_y.at[kz, ky - 1],
            send_sem=y_ss.at[kz, ky], recv_sem=y_rs.at[kz, ky],
            device_id=(z * n_y + to_y, m), device_id_type=MESH)

    def z_copy(kz):
        return pltpu.make_async_remote_copy(
            src_ref=send_z.at[kz - 1], dst_ref=recv_z.at[kz - 1], send_sem=z_ss.at[kz],
            recv_sem=z_rs.at[kz], device_id=(lax.rem(z + kz, n_z) * n_y + y, m),
            device_id_type=MESH)

    for kz in list(range(1, n_z)) + [0]:
        for ky in range(1, n_y):
            y_copy(kz, ky).start()

    def dp_ex(stage):
        return Exchange(n_dp, d, lambda p: (p, m), dp_ss.at[stage], dp_rs.at[stage])

    def mp_ex(stage):
        return Exchange(n_mp, m, lambda p: (d, p), mp_ss.at[stage], mp_rs.at[stage])

    def pair_sum(kz):
        for ky in range(1, n_y):
            y_copy(kz, ky).wait_recv()
        target = lax.rem(z + kz, n_z) * n_y + y
        value = grads_ref[:, pl.ds(pl.multiple_of(target * rows, rows), rows), :].astype(F32)
        for ky in range(1, n_y):
            value = value + recv_y[kz, ky - 1].astype(F32)
        return value

    def send_on(kz):
        send_z[kz - 1] = pair_sum(kz).astype(BF16)
        z_copy(kz).start()

    ex = mp_ex(0)
    ex.start(lambda p: dmods_ref, recv_q)
    recv_q[m] = dmods_ref[...]
    ex.wait(lambda p: dmods_ref, recv_q)
    own_q[...] = total_of(recv_q, n_mp)
    ex = dp_ex(0)
    ex.start(lambda p: own_q, recv_d)
    recv_d[d] = own_q[...]
    gains_own = emb_ref[d][images:]
    emb = emb_ref[:, 0:images, :]
    emb_factor = rms_blocks(emb)
    unit = emb * emb_factor[None] * emb_ref[:, images : images + 1, :]
    unit_factor = rms_blocks(unit)
    emb_own = emb_ref[d][0:images]
    unit_own = emb_own * emb_factor * gains_own[0:1]
    pre_own = (unit_own * unit_factor * gains_own[1:2]).astype(BF16)
    mixed = mixed_ref[...]
    mixed_factor = rms_blocks(mixed)
    mixed_own = mixed_ref[d]
    cond_own = (mixed_own * mixed_factor * gains_own[2:3]).astype(BF16)
    ex.wait(lambda p: own_q, recv_d)
    for p in range(n_dp):
        for c in range(2):
            full_d[c, p * IMG_DEV : (p + 1) * IMG_DEV, :] = recv_d[p, c]
    own_c[...] = two_part_left(dot_nt, full_d[0], wmod_ref[0]) + two_part_left(
        dot_nt, full_d[1], wmod_ref[1]
    )
    ex = dp_ex(1)
    ex.start(lambda p: own_c, recv_c)
    recv_c[d] = own_c[...]
    for c in range(2):
        gmod_ref[c] = two_part(dot_tn, cond_own, full_d[c])
    if n_z > 1:
        send_on(1)
    ex.wait(lambda p: own_c, recv_c)
    ggain_ref[2:3, :] = jnp.sum(own_c[...] * mixed_own * mixed_factor, axis=0, keepdims=True)
    d_mixed = rms_blocks_back(
        mixed, mixed_factor, recv_c[...] * emb_ref[:, images + 2 : images + 3, :]
    )
    recv_c[...] = d_mixed
    mix_own = recv_c[d]
    part = two_part_left(dot_nn, mix_own, wmd_ref[...])
    for p in range(n_dp):
        send_g[p] = part[p * IMG_DEV : (p + 1) * IMG_DEV, :]
    ex = dp_ex(2)
    ex.start(lambda p: send_g.at[p], recv_g)
    recv_g[d] = send_g[d]
    gmd_ref[...] = two_part_left(dot_tn, mix_own, gated_ref[...].astype(BF16))
    for kz in range(2, n_z):
        send_on(kz)
    ex.wait(lambda p: send_g.at[p], recv_g)
    d_gated = total_of(recv_g, n_dp)
    value, slope = gelu_parts(hid_ref[1])
    own_h[0] = d_gated * value
    own_h[1] = d_gated * hid_ref[0] * slope
    ex = dp_ex(3)
    ex.start(lambda p: own_h, recv_h)
    recv_h[d] = own_h[...]
    ex.wait(lambda p: own_h, recv_h)
    for p in range(n_dp):
        for c in range(2):
            full_h[c, p * IMG_DEV : (p + 1) * IMG_DEV, :] = recv_h[p, c]
    own_p[...] = two_part_left(dot_nt, full_h[0], wmu_ref[0]) + two_part_left(
        dot_nt, full_h[1], wmu_ref[1]
    )
    ex = mp_ex(1)
    ex.start(lambda p: own_p, recv_p)
    recv_p[m] = own_p[...]
    for c in range(2):
        gmu_ref[c] = two_part(dot_tn, pre_own, full_h[c])
    ex.wait(lambda p: own_p, recv_p)
    own_s[...] = total_of(recv_p, n_mp)
    ex = dp_ex(4)
    ex.start(lambda p: own_s, recv_s)
    recv_s[d] = own_s[...]
    gshard_ref[...] = pair_sum(0)
    ex.wait(lambda p: own_s, recv_s)
    ggain_ref[1:2, :] = jnp.sum(own_s[...] * unit_own * unit_factor, axis=0, keepdims=True)
    d_unit = recv_c[...] + rms_blocks_back(
        unit, unit_factor, recv_s[...] * emb_ref[:, images + 1 : images + 2, :]
    )
    recv_s[...] = d_unit
    ggain_ref[0:1, :] = jnp.sum(recv_s[d] * emb_own * emb_factor, axis=0, keepdims=True)
    d_emb = rms_blocks_back(emb, emb_factor, d_unit * emb_ref[:, images : images + 1, :])
    recv_s[...] = d_emb
    ggain_ref[3:8, :] = jnp.zeros_like(ggain_ref[3:8, :])
    for p in range(n_dp):
        gtime_ref[p] = two_part(dot_tn, feats_ref[...], recv_s[p])
    gclass_ref[...] = two_part_left(dot_tn, recv_s[d], onehot_ref[...])
    for kz in range(1, n_z):
        z_copy(kz).wait_recv()
        gshard_ref[...] = gshard_ref[...] + recv_z[kz - 1].astype(F32)
    for kz in range(1, n_z):
        z_copy(kz).wait_send()
    for kz in range(n_z):
        for ky in range(1, n_y):
            y_copy(kz, ky).wait_send()


def back(n_dp, n_mp, grads, dmods, feats_own, onehot, w_mapup, w_mapdown, w_mod, emb, hid, gated, mixed):
    images, part = feats_own.shape
    units = w_mapup.shape[2]
    n_y = minor_size(n_dp)
    n_z = n_dp // n_y
    rows = grads.shape[1] // n_dp
    slab = (grads.shape[0], rows, grads.shape[2])
    shape = lambda *dims: jax.ShapeDtypeStruct(dims, F32)
    return pl.pallas_call(
        functools.partial(back_kernel, n_dp, n_mp),
        out_shape=(
            shape(*slab),
            shape(2, part, D),
            shape(part, units),
            shape(2, part, units),
            shape(n_dp, part, part),
            shape(part, NCLASS),
            shape(8, part),
        ),
        in_specs=vmem_specs(11),
        out_specs=tuple(vmem_specs(7)),
        scratch_shapes=[
            pltpu.VMEM((n_mp, 2, IMG_DEV, D), F32),
            pltpu.VMEM((2, IMG_DEV, D), F32),
            pltpu.VMEM((n_dp, 2, IMG_DEV, D), F32),
            pltpu.VMEM((2, images, D), F32),
            pltpu.VMEM((images, part), F32),
            pltpu.VMEM((n_dp, images, part), F32),
            pltpu.VMEM((n_dp, IMG_DEV, units), F32),
            pltpu.VMEM((n_dp, IMG_DEV, units), F32),
            pltpu.VMEM((2, IMG_DEV, units), F32),
            pltpu.VMEM((n_dp, 2, IMG_DEV, units), F32),
            pltpu.VMEM((2, images, units), F32),
            pltpu.VMEM((images, part), F32),
            pltpu.VMEM((n_mp, images, part), F32),
            pltpu.VMEM((images, part), F32),
            pltpu.VMEM((n_dp, images, part), F32),
            pltpu.VMEM((n_z, max(n_y - 1, 1)) + slab, BF16),
            pltpu.VMEM((max(n_z - 1, 1),) + slab, BF16),
            pltpu.VMEM((max(n_z - 1, 1),) + slab, BF16),
            pltpu.SemaphoreType.DMA((5, n_dp)),
            pltpu.SemaphoreType.DMA((5, n_dp)),
            pltpu.SemaphoreType.DMA((2, n_mp)),
            pltpu.SemaphoreType.DMA((2, n_mp)),
            pltpu.SemaphoreType.DMA((n_z,)),
            pltpu.SemaphoreType.DMA((n_z,)),
            pltpu.SemaphoreType.DMA((n_z, n_y)),
            pltpu.SemaphoreType.DMA((n_z, n_y)),
        ],
        compiler_params=pltpu.CompilerParams(
            collective_id=1, has_side_effects=True, vmem_limit_bytes=VMEM_BYTES
        ),
        name="back",
    )(grads, dmods, feats_own, onehot, w_mapup, w_mapdown, w_mod, emb, hid, gated, mixed)


def norm_kernel(n_dp, n_mp, heads, v_ref, o_ref, own, recv_dp, recv_mp, dp_ss, dp_rs, mp_ss, mp_rs):
    d, m = lax.axis_index("dp"), lax.axis_index("mp")
    greet(
        [
            (n_dp, lambda k: (lax.rem(d + k, n_dp), m)),
            (n_mp, lambda k: (d, lax.rem(m + k, n_mp))),
        ]
    )
    ex = Exchange(n_dp, d, lambda p: (p, m), dp_ss, dp_rs)
    ex.start(lambda p: v_ref, recv_dp)
    recv_dp[d] = v_ref[...]
    ex.wait(lambda p: v_ref, recv_dp)
    summed = total_of(recv_dp, n_dp)
    head = summed[1:2]
    squares = summed[0:1] + head * head
    own[...] = jnp.zeros_like(own)
    own[0:1, :] = squares
    ex = Exchange(n_mp, m, lambda p: (d, p), mp_ss, mp_rs)
    ex.start(lambda p: own, recv_mp)
    recv_mp[m] = own[...]
    ex.wait(lambda p: own, recv_mp)
    norm = jnp.sqrt(jnp.sum(total_of(recv_mp, n_mp)[0:1], axis=-1, keepdims=True))
    o_ref[...] = jnp.zeros_like(o_ref)
    o_ref[0:1, :] = jnp.broadcast_to(norm, (1, o_ref.shape[1]))
    o_ref[1:2, :] = head


def norm_all(n_dp, n_mp, heads, values):
    return pl.pallas_call(
        functools.partial(norm_kernel, n_dp, n_mp, heads),
        out_shape=jax.ShapeDtypeStruct(values.shape, F32),
        in_specs=vmem_specs(1),
        out_specs=vmem_specs(1)[0],
        scratch_shapes=[
            pltpu.VMEM(values.shape, F32),
            pltpu.VMEM((n_dp,) + values.shape, F32),
            pltpu.VMEM((n_mp,) + values.shape, F32),
            pltpu.SemaphoreType.DMA((n_dp,)),
            pltpu.SemaphoreType.DMA((n_dp,)),
            pltpu.SemaphoreType.DMA((n_mp,)),
            pltpu.SemaphoreType.DMA((n_mp,)),
        ],
        compiler_params=pltpu.CompilerParams(collective_id=2, has_side_effects=True),
        name="norm_all",
    )(values)


def rms_scale(values, scales):
    return values * lax.rsqrt(jnp.mean(values * values, axis=-1, keepdims=True) + EPSILON) * scales


def geglu_gate(hidden):
    return hidden[:, 0] * jax.nn.gelu(hidden[:, 1], approximate=False)


def cosine(queries, key_rows, head_scale):
    query_unit = (
        queries
        * lax.rsqrt(jnp.sum(queries * queries, axis=-1, keepdims=True) + EPSILON)
        * head_scale[None, :, None]
    )
    key_unit = key_rows * lax.rsqrt(jnp.sum(key_rows * key_rows, axis=-1, keepdims=True) + EPSILON)
    return (query_unit, key_unit)


def middle_part(block_input, out_cotangent, mods, my_lengths, wg, wf, head_scale):
    n_dp = lax.axis_size("dp")
    w_in = jnp.transpose(wg[:3], (1, 0, 2))
    w_out = wg[3].T
    rows = D // n_dp
    w_up = jnp.transpose(wf.reshape(n_dp, 3, rows, -1)[:, :2], (0, 2, 1, 3)).reshape(D, 2, -1)
    w_down = wf.reshape(n_dp, 3, rows, -1)[:, 2].reshape(D, -1).T
    slot_count = block_input.shape[0]
    image_ends = jnp.cumsum(my_lengths)
    position = jnp.arange(slot_count, dtype=jnp.int32)
    slot_of = jnp.sum((position[:, None] >= image_ends[None, :]).astype(jnp.int32), axis=1)
    live_rows = (position < image_ends[-1]).astype(jnp.float32)[:, None]
    member = (slot_of[:, None] == jnp.arange(IMG_DEV, dtype=jnp.int32)[None, :]).astype(jnp.float32)
    same_image = slot_of[:, None] == slot_of[None, :]
    hi = lax.Precision.HIGHEST
    attn_mod = 1.0 + jnp.dot(member, mods[0], precision=hi)
    ff_mod = 1.0 + jnp.dot(member, mods[1], precision=hi)
    heads_here = head_scale.shape[0]
    width_here = w_in.shape[2]
    head_size = width_here // heads_here
    inputs = block_input.astype(jnp.float32)
    normed_in, in_back = jax.vjp(rms_scale, inputs, attn_mod)
    low_in = normed_in.astype(jnp.bfloat16)
    projected = jnp.einsum("td,dcf->tcf", low_in, w_in, preferred_element_type=jnp.float32)
    queries = projected[:, 0].reshape(slot_count, heads_here, head_size)
    key_rows = projected[:, 1].reshape(slot_count, heads_here, head_size)
    (query_unit, key_unit), cosine_back = jax.vjp(cosine, queries, key_rows, head_scale)
    query_low = query_unit.astype(jnp.bfloat16)
    key_low = key_unit.astype(jnp.bfloat16)
    value_low = projected[:, 2].reshape(slot_count, heads_here, head_size).astype(jnp.bfloat16)
    scores = jnp.einsum("thd,uhd->htu", query_low, key_low, preferred_element_type=jnp.float32)
    scores = jnp.where(same_image[None], scores, MASKED)
    row_max = jnp.max(scores, axis=-1, keepdims=True)
    expon = jnp.exp(scores - row_max)
    row_total = jnp.sum(expon, axis=-1, keepdims=True)
    probabilities = expon / row_total
    log_total = row_max + jnp.log(row_total)
    attended = jnp.einsum(
        "htu,uhd->thd",
        probabilities.astype(jnp.bfloat16),
        value_low,
        preferred_element_type=jnp.float32,
    )
    attended_low = attended.reshape(slot_count, width_here).astype(jnp.bfloat16)
    branch_attn = lax.psum(jnp.dot(attended_low, w_out, preferred_element_type=jnp.float32), "mp")
    middle = inputs + branch_attn
    normed_mid, mid_back = jax.vjp(rms_scale, middle, ff_mod)
    low_mid = normed_mid.astype(jnp.bfloat16)
    hidden = jnp.einsum("td,dcf->tcf", low_mid, w_up, preferred_element_type=jnp.float32)
    gated_vals, gate_back = jax.vjp(geglu_gate, hidden)
    gated_low = gated_vals.astype(jnp.bfloat16)
    branch_ff = lax.psum(
        jnp.dot(gated_low, w_down, preferred_element_type=jnp.float32).astype(jnp.bfloat16), "mp"
    ).astype(jnp.float32)
    layer_out = (live_rows * (middle + branch_ff)).astype(jnp.bfloat16)
    out_grad = live_rows * out_cotangent.astype(jnp.float32)
    grad_branch = out_grad.astype(jnp.bfloat16)
    grad_downproj = jnp.dot(gated_low.T, grad_branch, preferred_element_type=jnp.float32)
    grad_gated = jnp.dot(grad_branch, w_down.T, preferred_element_type=jnp.float32)
    (grad_hidden,) = gate_back(grad_gated)
    grad_hidden_low = grad_hidden.astype(jnp.bfloat16)
    grad_upproj = jnp.einsum(
        "td,tcf->dcf", low_mid, grad_hidden_low, preferred_element_type=jnp.float32
    )
    grad_low_mid = lax.psum(
        jnp.einsum("tcf,dcf->td", grad_hidden_low, w_up, preferred_element_type=jnp.float32), "mp"
    )
    grad_mid_norm, grad_ff_mod = mid_back(grad_low_mid)
    grad_middle = out_grad + grad_mid_norm
    grad_y = grad_middle.astype(jnp.bfloat16)
    grad_outproj = jnp.dot(attended_low.T, grad_y, preferred_element_type=jnp.float32)
    grad_att = (
        jnp.dot(grad_y, w_out.T, preferred_element_type=jnp.float32)
        .astype(jnp.bfloat16)
        .reshape(slot_count, heads_here, head_size)
    )
    again = jnp.einsum("thd,uhd->htu", query_low, key_low, preferred_element_type=jnp.float32)
    again = jnp.where(same_image[None], again, MASKED)
    probs_again = jnp.exp(again - log_total)
    grad_values = jnp.einsum(
        "htu,thd->uhd",
        probs_again.astype(jnp.bfloat16),
        grad_att,
        preferred_element_type=jnp.float32,
    )
    grad_probs = jnp.einsum("thd,uhd->htu", grad_att, value_low, preferred_element_type=jnp.float32)
    inner = jnp.sum(grad_probs * probs_again, axis=-1, keepdims=True)
    grad_scores = (probs_again * (grad_probs - inner)).astype(jnp.bfloat16)
    grad_qunit = jnp.einsum(
        "htu,uhd->thd", grad_scores, key_low, preferred_element_type=jnp.float32
    )
    grad_kunit = jnp.einsum(
        "htu,thd->uhd", grad_scores, query_low, preferred_element_type=jnp.float32
    )
    grad_queries, grad_keys, grad_headscale = cosine_back((grad_qunit, grad_kunit))
    grad_projected = jnp.stack(
        [
            grad_queries.reshape(slot_count, width_here),
            grad_keys.reshape(slot_count, width_here),
            grad_values.reshape(slot_count, width_here),
        ],
        axis=1,
    ).astype(jnp.bfloat16)
    grad_inproj = jnp.einsum(
        "td,tcf->dcf", low_in, grad_projected, preferred_element_type=jnp.float32
    )
    grad_low_in = lax.psum(
        jnp.einsum("tcf,dcf->td", grad_projected, w_in, preferred_element_type=jnp.float32), "mp"
    )
    grad_in_norm, grad_attn_mod = in_back(grad_low_in)
    input_grad = grad_middle + grad_in_norm
    grad_mods = jnp.stack(
        [
            jnp.dot(member.T, grad_attn_mod, precision=hi),
            jnp.dot(member.T, grad_ff_mod, precision=hi),
        ],
        axis=0,
    ) / lax.axis_size("mp")
    grad_attn_w = jnp.concatenate(
        [jnp.transpose(grad_inproj, (1, 0, 2)), grad_outproj.T[None]], axis=0
    ).astype(BF16)
    grad_ffn_w = jnp.concatenate(
        [
            jnp.transpose(grad_upproj, (1, 0, 2)).reshape(2, n_dp, rows, -1),
            grad_downproj.T.reshape(1, n_dp, rows, -1),
        ],
        axis=0,
    ).astype(BF16)
    grad_ffn_w = jnp.transpose(grad_ffn_w, (1, 0, 2, 3)).reshape(n_dp, 3 * rows, -1)
    return layer_out, input_grad, grad_mods, grad_attn_w, grad_ffn_w, grad_headscale


def per_device(
    block_input,
    out_cotangent,
    sigmas,
    class_labels,
    image_lengths,
    fourier_freqs,
    inproj_state,
    outproj_state,
    upproj_state,
    downproj_state,
    timeproj_state,
    classemb_state,
    mapup_state,
    mapdown_state,
    modproj_state,
    gains_state,
    headscale_state,
):
    n_dp, n_mp = lax.axis_size("dp"), lax.axis_size("mp")
    d = lax.axis_index("dp")
    my_lengths = lax.dynamic_slice_in_dim(image_lengths, d * IMG_DEV, IMG_DEV)
    rows, _, width = inproj_state.shape[1:]
    units = upproj_state.shape[3]
    part = timeproj_state.shape[1]
    ffn_shard = jnp.concatenate(
        [
            jnp.transpose(upproj_state[0].astype(BF16), (1, 0, 2)).reshape(2 * rows, units),
            downproj_state[0].astype(BF16).T,
        ],
        axis=0,
    )
    wf = lax.all_gather(ffn_shard, "dp", axis=0)
    attn_shard = jnp.concatenate(
        [
            jnp.transpose(inproj_state[0].astype(BF16), (1, 0, 2)),
            outproj_state[0].astype(BF16).T[None],
        ],
        axis=0,
    )
    feats_low = fourier(sigmas, fourier_freqs).astype(BF16)
    feats_own = lax.dynamic_slice_in_dim(feats_low, d * part, part, axis=1)
    onehot = (class_labels[:, None] == jnp.arange(NCLASS, dtype=jnp.int32)[None, :]).astype(BF16)
    e_cols = dot_nt(onehot, classemb_state[0].astype(BF16).T)
    gains_own = jnp.pad(gains_state[0].astype(BF16).astype(F32), ((0, 5), (0, 0)))
    w_time = jnp.transpose(timeproj_state[0].astype(BF16).reshape(part, n_dp, part), (1, 0, 2))
    w_mapup = jnp.transpose(mapup_state[0].astype(BF16), (1, 0, 2))
    w_mapdown = mapdown_state[0].astype(BF16).T
    w_mod = jnp.transpose(modproj_state[0].astype(BF16), (1, 0, 2))
    wg, mods, emb, hid, gated, mixed = front(
        n_dp, n_mp, attn_shard, feats_own, w_time, e_cols, gains_own, w_mapup, w_mapdown, w_mod
    )
    layer_out, input_grad, grad_mods, grad_attn_w, grad_ffn_w, grad_headscale = middle_part(
        block_input, out_cotangent, mods, my_lengths, wg, wf, headscale_state[0]
    )
    g_ffn = lax.psum_scatter(grad_ffn_w, "dp", scatter_dimension=0).astype(F32)
    g_attn, g_mod, g_md, g_mu, g_time, g_class, g_gain = back(
        n_dp, n_mp, grad_attn_w, grad_mods, feats_own, onehot, w_mapup, w_mapdown, w_mod, emb, hid, gated, mixed
    )
    g_gain = g_gain[:3]
    g_ffn = g_ffn.reshape(3, rows, units)
    split = jnp.sum(g_attn * g_attn) + jnp.sum(g_ffn * g_ffn) + jnp.sum(g_mu * g_mu) + jnp.sum(g_md * g_md)
    shared = (
        jnp.sum(g_mod * g_mod) + jnp.sum(g_time * g_time) + jnp.sum(g_class * g_class) + jnp.sum(g_gain * g_gain)
    )
    heads_here = headscale_state.shape[1]
    packed = jnp.zeros((8, 128), F32).at[0, 0].set(split + shared / n_mp).at[1, :heads_here].set(grad_headscale)
    normed = norm_all(n_dp, n_mp, heads_here, packed)
    grad_norm = normed[0, 0]
    factor = CLIP_NORM / jnp.maximum(grad_norm, CLIP_NORM)
    gradients = (
        jnp.transpose(g_attn[:3], (1, 0, 2)),
        g_attn[3].T,
        jnp.transpose(g_ffn[:2], (1, 0, 2)),
        g_ffn[2].T,
        jnp.transpose(g_time, (1, 0, 2)).reshape(part, DM),
        g_class.T,
        jnp.transpose(g_mu, (1, 0, 2)),
        g_md.T,
        jnp.transpose(g_mod, (1, 0, 2)),
        g_gain,
        normed[1, :heads_here],
    )
    states = (
        inproj_state,
        outproj_state,
        upproj_state,
        downproj_state,
        timeproj_state,
        classemb_state,
        mapup_state,
        mapdown_state,
        modproj_state,
        gains_state,
        headscale_state,
    )
    rates = learn_rates()
    decays = decay_rates()
    results = [layer_out, input_grad, grad_norm]
    for index in range(11):
        results += adamw_step(states[index], factor * gradients[index], rates[index], decays[index])
    return tuple(results)


def solution(mesh):
    return jax.shard_map(
        per_device,
        mesh=mesh,
        in_specs=(
            P("dp", None),
            P("dp", None),
            P(),
            P(),
            P(),
            P(),
            P(None, "dp", None, "mp"),
            P(None, "mp", "dp"),
            P(None, "dp", None, "mp"),
            P(None, "mp", "dp"),
            P(None, "dp", None),
            P(None, None, "dp"),
            P(None, "dp", None, "mp"),
            P(None, "mp", "dp"),
            P(None, "dp", None, None),
            P(None, None, "dp"),
            P(None, "mp"),
        ),
        out_specs=(
            P("dp", None),
            P("dp", None),
            P(),
            P(None, "dp", None, "mp"),
            P("dp", None, "mp"),
            P("dp", None, "mp"),
            P(None, "mp", "dp"),
            P("mp", "dp"),
            P("mp", "dp"),
            P(None, "dp", None, "mp"),
            P("dp", None, "mp"),
            P("dp", None, "mp"),
            P(None, "mp", "dp"),
            P("mp", "dp"),
            P("mp", "dp"),
            P(None, "dp", None),
            P("dp", None),
            P("dp", None),
            P(None, None, "dp"),
            P(None, "dp"),
            P(None, "dp"),
            P(None, "dp", None, "mp"),
            P("dp", None, "mp"),
            P("dp", None, "mp"),
            P(None, "mp", "dp"),
            P("mp", "dp"),
            P("mp", "dp"),
            P(None, "dp", None, None),
            P("dp", None, None),
            P("dp", None, None),
            P(None, None, "dp"),
            P(None, "dp"),
            P(None, "dp"),
            P(None, "mp"),
            P("mp"),
            P("mp"),
        ),
        check_vma=False,
    )
```

time: 1790 us -> 769 us (0.43)
  waiting for transfers between devices: 1250 us -> 234 us
  Pallas kernels: 0 us -> 167 us
  blocking collectives: 148 us -> 0 us
  matrix products: 154 us -> 105 us
  other arithmetic: 110 us -> 128 us
    reduce_scatter x8 -> x1, waiting for transfers between devices: 598 us -> 0.01 us  [per_device(): g_ffn = lax.psum_scatter(grad_ffn_w, 'dp', scatter_dimension=0).astype(F32)]
    unnamed x23 -> x6, waiting for transfers between devices: 200 us -> 0.1 us
    all_gather x7 -> x1, waiting for transfers between devices: 174 us -> 0.03 us  [per_device(): wf = lax.all_gather(ffn_shard, 'dp', axis=0)]
    pallas_call x0 -> x3, Pallas kernels: none -> 167 us  [the longest x1 81 us: front(): pl.pallas_call(functools.partial(front_kernel, n_dp, n_mp), out_shape=(ja...]
    all_gather x3 -> x0, blocking collectives: 86.5 us -> none  [the longest x1 34.9 us: per_device(): lax.all_gather(mapdown_state[0].astype(jnp.bfloat16), 'dp', axis=1, tiled...]
    psum x3 -> x0, blocking collectives: 61.3 us -> none  [the longest x1 39.6 us: per_device(): squares_all, head_total = lax.psum((squares, head_full), ('dp', 'mp'))]
    dot_general x35 -> x23, matrix products: 154 us -> 105 us  [the longest x1 15.3 us: middle_part(): jnp.einsum('thd,uhd->htu', grad_att, value_low, preferred_element_type=jn...]
    psum x4, waiting for transfers between devices: 278 us -> 234 us  [the longest x1 72.3 us: middle_part(): lax.psum(jnp.einsum('tcf,dcf->td', grad_hidden_low, w_up, preferred_eleme...]
  transfers between devices with their start and end apart: 21 -> 6, of which waited for: 17 -> 4; matrix products, arithmetic and copies ran while one was open for 11% -> 14% of each run, Pallas kernels for 0% -> 10%
where the time goes in v1:
time: 769 us; the launch traced here: 758 us
  waiting for transfers between devices  234 us (30%)
  Pallas kernels  167 us (22%)
  other arithmetic  128 us (17%)
  matrix products  105 us (14%)
  local copies, waits for them, and re-layouts  101 us (13%)
  between operations  22.7 us (3%)
    pallas_call x1, Pallas kernels, front(): pl.pallas_call(functools.partial(front_kernel, n_dp, n_mp), out_shape=(ja...  81 us
    pallas_call x1, Pallas kernels, back(): pl.pallas_call(functools.partial(back_kernel, n_dp, n_mp), out_shape=(sha...  76.5 us
    psum x1, waiting for transfers between devices, middle_part(): lax.psum(jnp.einsum('tcf,dcf->td', grad_hidden_low, w_up, preferred_eleme...  72.3 us
    unnamed x286, local copies, waits for them, and re-layouts  67.6 us
    psum x1, waiting for transfers between devices, middle_part(): lax.psum(jnp.dot(attended_low, w_out, preferred_element_type=jnp.float32)...  61.2 us
    psum x1, waiting for transfers between devices, middle_part(): lax.psum(jnp.einsum('tcf,dcf->td', grad_projected, w_in, preferred_elemen...  52.5 us
    psum x1, waiting for transfers between devices, middle_part(): lax.psum(jnp.dot(gated_low, w_down, preferred_element_type=jnp.float32).a...  48.2 us
    another operation x22, other arithmetic, adamw_step(): return (jnp.stack([weight, average]), first, second)  23.6 us
  transfers between devices with their start and end apart: 6, of which 4 were waited for; matrix products, arithmetic and copies ran while one was open for 14% of the time, Pallas kernels for 10%

profile of v1, /device:TPU:0, one launch (start us, length us, event | category | flops | bytes accessed | tf_op | source)
XLA Modules:
  0.0 758.2 jit_solution(10491314986114946538)
XLA Ops:
  27.2 3.9 fusion.198
  36.4 81.0 %front.1 = (bf16[4,1024,256]{2,1,0:T(8,128)(2,1)}, f32[2,4,1024]{2,1,0:T(4,128)}, f32[8,40,96]{2,1,0:T(8,128)}, f32[2,4,576]{2,1,0:T(4,128)}, f32[32,576]{1,0:T(8,128)}, /*index=5*/f32[8,32,96]{2,1,0:T(8,128)}) custom-call(bf16[4,128,256]{2,1,0:T(8,128)(2,1)} %pad_maximum_fusion.14.shard_ref, bf16[32,96]{1,0:T(8,128)(2,1)} %fusion.154.feats_ref, ...), custom_call_target="tpu_custom_call" | custom-call | tf_op jit(solution)/shard_map/front/pallas_call | solution.py:324
  127.4 7.5 select_reduce_fusion
  134.9 9.0 %fusion = f32[4,1024]{1,0:T(4,128)S(1)} fusion(f32[4,1024,1024]{1,2,0:T(8,128)} %get-tuple-element.273, f32[4,1024]{1,0:T(4,128)S(1)} %get-tuple-element.272, pred[1024,1024]{0,1:T(8,128)(4,1)} %broadcast_compare_fusion), kind=kLoop, calls=%fused_computation.5 | loop fusion | flops 12578816 | bytes 17858560 | tf_op jit(solution)/shard_map/reduce_sum | solution.py:681
  144.0 8.3 %fusion.69 = bf16[4,64,1024]{2,1,0:T(8,128)(2,1)S(1)} fusion(bf16[1024,4,64]{0,2,1:T(8,128)(2,1)} %bitcast.505, f32[4,1024,1024]{1,2,0:T(8,128)} %get-tuple-element.273, f32[4,1024]{1,0:T(4,128)S(1)} %fusion, f32[4,1024]{1,0:T(4,128)S(1)} %get-tuple-element.272, pred[1024,1024]{0,1:T(8,128)(4,1)} %broadcast_compare_fusion), kind=kOutput, calls=%fused_computation.121 | convolution fusion | flops 553910272 | bytes 18907136 | tf_op jit(solution)/shard_map/htu,uhd->thd/dot_general | solution.py:684
  153.2 3.8 fusion.96
  160.7 4.3 fusion.199
  167.5 4.1 copy.179
  172.3 3.7 fusion.17
  176.0 3.9 fusion.99
  179.9 61.2 %all-reduce.9.cloned.1.call-done = f32[1024,1024]{0,1:T(8,128)} async-done(((f32[1024,1024]{0,1:T(8,128)}), f32[1024,1024]{0,1:T(8,128)}) %all-reduce.9.cloned.1.call-update) | async-done | bytes 4194320 | tf_op jit(solution)/shard_map/psum | solution.py:691
  256.2 3.6 fusion.205
  259.8 7.7 %fusion.30 = (f32[1024,1,768]{2,0,1:T(8,128)S(1)}, f32[1024,768]{1,0:T(8,128)S(1)}) fusion(f32[1024,768]{1,0:T(8,128)S(1)} %fusion.206, f32[1024,2,768]{2,0,1:T(8,128)S(1)} %fusion.205), kind=kLoop, calls=%fused_computation.60 | loop fusion | flops 56623104 | bytes 15728640 | tf_op jit(solution)/shard_map/transpose(jvp())/broadcast_in_dim | solution.py:634
  270.1 5.0 convolution_bitcast_fusion.1
  275.2 8.4 %fusion.22 = bf16[1024,1,768]{2,0,1:T(8,128)(2,1)S(1)} fusion(f32[1024,2,768]{2,0,1:T(8,128)} %copy-done.12), kind=kLoop, calls=%fused_computation.44 | loop fusion | flops 51904512 | bytes 7864320 | tf_op jit(solution)/shard_map/convert_element_type | solution.py:697
  288.6 72.3 %all-reduce.13.cloned.1.call-done = f32[1024,1024]{0,1:T(8,128)} async-done(((f32[1024,1024]{0,1:T(8,128)}), f32[1024,1024]{0,1:T(8,128)}) %all-reduce.13.cloned.1.call-update) | async-done | bytes 4194320 | tf_op jit(solution)/shard_map/psum | solution.py:711
  360.9 5.7 multiply_reduce_fusion.1
  366.6 48.2 %all-reduce.11.cloned.1.call-done = bf16[1024,1024]{0,1:T(8,128)(2,1)} async-done(((bf16[1024,1024]{0,1:T(8,128)(2,1)}), bf16[1024,1024]{0,1:T(8,128)(2,1)}) %all-reduce.11.cloned.1.call-update) | async-done | bytes 2097168 | tf_op jit(solution)/shard_map/psum | solution.py:698
  414.8 7.8 %fusion.11 = (f32[1024,1024]{0,1:T(8,128)S(1)}, bf16[1024,1024]{0,1:T(8,128)(2,1)}) fusion(f32[1024,1024]{0,1:T(8,128)} %copy-done.2, bf16[1024,1024]{0,1:T(8,128)(2,1)S(1)} %copy-done.18, f32[1024]{0:T(1024)S(1)} %multiply_multiply_fusion.18, f32[1024]{0:T(1024)S(1)} %fusion.157, f32[1024]{0:T(1024)S(1)} %fusion.155, ...), kind=kLoop, calls=%fused_computation.26 | loop fusion | flops 13631488 | bytes 23080960 | tf_op jit(solution)/shard_map/add | solution.py:715
  425.7 8.8 %fusion.66 = bf16[4,64,1024]{2,1,0:T(8,128)(2,1)} fusion(bf16[1024,4,64]{0,2,1:T(8,128)(2,1)S(1)} %bitcast.503, f32[4,1024,1024]{1,2,0:T(8,128)} %get-tuple-element.273, f32[4,1024]{1,0:T(4,128)S(1)} %copy-done.97, pred[1024,1024]{0,1:T(8,128)(4,1)S(1)} %copy-done.17), kind=kOutput, calls=%fused_computation.118 | convolution fusion | flops 549715968 | bytes 18890752 | tf_op jit(solution)/shard_map/htu,thd->uhd/dot_general | solution.py:726
  434.6 15.3 %multiply_reduce_fusion = (f32[4,1024]{1,0:T(4,128)}, f32[4,1024,1024]{1,2,0:T(8,128)}) fusion(f32[4,1024,1024]{1,2,0:T(8,128)} %get-tuple-element.273, f32[4,1024]{1,0:T(4,128)} %log_add_fusion, pred[1024,1024]{0,1:T(8,128)(4,1)} %broadcast_compare_fusion, bf16[1024,4,64]{0,2,1:T(8,128)(2,1)} %bitcast.504, bf16[1024,4,64]{0,2,1:T(8,128)(2,1)} %bitcast.506), kind=kOutput, calls=%fused_computation.1 | convolution fusion | flops 553644032 | bytes 35684352 | tf_op jit(solution)/shard_map/thd,uhd->htu/dot_general | solution.py:732
  449.8 10.9 %multiply_convert_fusion = bf16[4,1024,1024]{1,2,0:T(8,128)(2,1)} fusion(f32[4,1024,1024]{1,2,0:T(8,128)} %get-tuple-element.275, f32[4,1024,1024]{1,2,0:T(8,128)S(1)} %bitcast.479, f32[4,1024]{1,0:T(4,128)} %get-tuple-element.274, f32[4,1024]{1,0:T(4,128)} %log_add_fusion, pred[1024,1024]{0,1:T(8,128)(4,1)} %broadcast_compare_fusion), kind=kLoop, calls=%fused_computation | loop fusion | flops 20971520 | bytes 43024384 | tf_op jit(solution)/shard_map/convert_element_type | solution.py:734
  460.8 7.5 multiply_reduce_fusion.5
  477.9 5.3 convolution_bitcast_fusion
  488.7 4.2 convolution_convert_fusion
  516.4 52.5 %all-reduce.15.cloned.1.call-done = f32[1024,1024]{0,1:T(8,128)} async-done(((f32[1024,1024]{0,1:T(8,128)}), f32[1024,1024]{0,1:T(8,128)}) %all-reduce.15.cloned.1.call-update) | async-done | bytes 4194320 | tf_op jit(solution)/shard_map/psum | solution.py:753
  568.9 4.8 fusion.14
  574.9 5.6 fusion.12
  580.5 5.5 copy.211
  586.0 4.7 fusion.74
  591.4 76.5 %back.1 = (f32[4,128,256]{2,1,0:T(8,128)}, f32[2,96,1024]{2,1,0:T(8,128)}, f32[96,576]{1,0:T(8,128)}, f32[2,96,576]{2,1,0:T(8,128)}, f32[8,96,96]{2,1,0:T(8,128)}, /*index=5*/f32[96,1000]{1,0:T(8,128)}, f32[8,96]{1,0:T(8,128)}) custom-call(bf16[4,1024,256]{2,1,0:T(8,128)(2,1)} %pad_maximum_fusion.1.grads_ref, f32[2,4,1024]{2,1,0:T(4,128)} %maximum_multiply_fusion.dmods_ref, ...), custom_call_target="tpu_custom_call" | custom-call | tf_op jit(solution)/shard_map/back/pallas_call | solution.py:534
  687.9 9.9 %norm_all.1 = f32[8,128]{1,0:T(8,128)} custom-call(f32[8,128]{1,0:T(8,128)} %copy-done.111), custom_call_target="tpu_custom_call" | custom-call | tf_op jit(solution)/shard_map/norm_all/pallas_call | solution.py:610
  (406 shorter events, 174.4 us)
Async XLA Ops:
  8.1 11.9 %copy-start.56 = (f32[4,96,2,576]{3,2,1,0:T(2,128)S(1)}, f32[4,96,2,576]{3,2,1,0:T(2,128)}, u32[]{:S(2)}) copy-start(f32[4,96,2,576]{3,2,1,0:T(2,128)} %param.33) | copy-start | bytes 5308420
  8.1 233.1 %all-reduce.9.cloned.1.call-start = ((), (), s32[]{:S(2)}) async-start(), calls=%async_computation.1 | async-start | bytes 8388608 | tf_op jit(solution)/shard_map/psum | solution.py:691
  25.8 215.3 %copy-start.4 = (bf16[1024,1024]{0,1:T(8,128)(2,1)}, bf16[1024,1024]{0,1:T(8,128)(2,1)S(1)}, u32[]{:S(2)}) copy-start(bf16[1024,1024]{0,1:T(8,128)(2,1)S(1)} %copy.164) | copy-start | bytes 6291460
  27.1 92.9 %copy-start.106 = (f32[1024]{0:T(1024)}, f32[1024]{0:T(1024)S(1)}, u32[]{:S(2)}) copy-start(f32[1024]{0:T(1024)S(1)} %fusion.156) | copy-start | bytes 12292
  126.2 8.7 %copy-start.13 = (f32[1024,1,256]{0,2,1:T(8,128)}, f32[1024,1,256]{0,2,1:T(8,128)S(1)}, u32[]{:S(2)}) copy-start(f32[1024,1,256]{0,2,1:T(8,128)S(1)} %get-tuple-element.248) | copy-start | bytes 3145732
  127.2 7.7 %copy-start.98 = (f32[1024,4]{0,1:T(4,128)}, f32[1024,4]{0,1:T(4,128)S(1)}, u32[]{:S(2)}) copy-start(f32[1024,4]{0,1:T(4,128)S(1)} %multiply_reduce_fusion.7) | copy-start | bytes 49156
  127.3 7.6 %copy-start.100 = (f32[1024,4]{0,1:T(4,128)}, f32[1024,4]{0,1:T(4,128)S(1)}, u32[]{:S(2)}) copy-start(f32[1024,4]{0,1:T(4,128)S(1)} %multiply_reduce_fusion.8) | copy-start | bytes 49156
  127.3 7.6 copy-start.78
  127.3 7.6 copy-start.83
  134.9 9.1 %copy-start.102 = (f32[4,1024]{1,0:T(4,128)}, f32[4,1024]{1,0:T(4,128)S(1)}, u32[]{:S(2)}) copy-start(f32[4,1024]{1,0:T(4,128)S(1)} %get-tuple-element.272) | copy-start | bytes 49156
  144.0 8.4 %copy-start.104 = (f32[4,1024]{1,0:T(4,128)}, f32[4,1024]{1,0:T(4,128)S(1)}, u32[]{:S(2)}) copy-start(f32[4,1024]{1,0:T(4,128)S(1)} %fusion) | copy-start | bytes 49156
  156.9 90.7 %all-gather.3.cloned.1.call-start = ((), (), s32[]{:S(2)}) async-start(), calls=%async_computation.6 | async-start | bytes 5308416 | tf_op jit(solution)/shard_map/all_gather | solution.py:811
  166.8 194.1 %all-reduce.13.cloned.1.call-start = ((), (), s32[]{:S(2)}) async-start(), calls=%async_computation.3 | async-start | bytes 8388608 | tf_op jit(solution)/shard_map/psum | solution.py:711
  247.6 8.6 %copy-start.45 = (bf16[1024,1024,1]{0,1,2:T(8,128)(2,1)}, bf16[1024,1024,1]{0,1,2:T(8,128)(2,1)S(1)}, u32[]{:S(2)}) copy-start(bf16[1024,1024,1]{0,1,2:T(8,128)(2,1)S(1)} %fusion.51) | copy-start | bytes 6291460
  259.8 7.7 %copy-start.12 = (f32[1024,2,768]{2,0,1:T(8,128)}, f32[1024,2,768]{2,0,1:T(8,128)S(1)}, u32[]{:S(2)}) copy-start(f32[1024,2,768]{2,0,1:T(8,128)S(1)} %fusion.205) | copy-start | bytes 18874372
  275.1 9.7 %copy-start.64 = (bf16[8,1,128,768]{3,2,1,0:T(8,128)(2,1)S(1)}, bf16[8,1,128,768]{3,2,1,0:T(8,128)(2,1)}, u32[]{:S(2)}) copy-start(bf16[8,1,128,768]{3,2,1,0:T(8,128)(2,1)} %copy-done.63) | copy-start | bytes 4718596
  275.1 139.7 %all-reduce.11.cloned.1.call-start = ((), (), s32[]{:S(2)}) async-start(), calls=%async_computation.2 | async-start | bytes 4194304 | tf_op jit(solution)/shard_map/psum | solution.py:698
  287.9 281.0 %all-reduce.15.cloned.1.call-start = ((), (), s32[]{:S(2)}) async-start(), calls=%async_computation.4 | async-start | bytes 8388608 | tf_op jit(solution)/shard_map/psum | solution.py:753
  288.6 126.2 %copy-start.18 = (bf16[1024,1024]{0,1:T(8,128)(2,1)S(1)}, bf16[1024,1024]{0,1:T(8,128)(2,1)}, u32[]{:S(2)}) copy-start(bf16[1024,1024]{0,1:T(8,128)(2,1)} %copy.179) | copy-start | bytes 6291460
  425.7 24.1 %slice-start = ((s8[16777216]{0:T(1024)(128)(4,1)}), s8[4194304]{0:T(1024)(128)(4,1)S(1)}, s32[]{:S(2)}) async-start(s8[16777216]{0:T(1024)(128)(4,1)} %bitcast.478), calls=%async_computation.7 | async-start | bytes 8388608
  425.7 24.1 %slice-start.1 = ((s8[16777216]{0:T(1024)(128)(4,1)}), s8[4194304]{0:T(1024)(128)(4,1)S(1)}, s32[]{:S(2)}) async-start(s8[16777216]{0:T(1024)(128)(4,1)} %bitcast.478), calls=%async_computation.8 | async-start | bytes 8388608
  434.6 15.3 %slice-start.2 = ((s8[16777216]{0:T(1024)(128)(4,1)}), s8[4194304]{0:T(1024)(128)(4,1)S(1)}, s32[]{:S(2)}) async-start(s8[16777216]{0:T(1024)(128)(4,1)} %bitcast.478), calls=%async_computation.9 | async-start | bytes 8388608
  434.6 15.3 %slice-start.3 = ((s8[16777216]{0:T(1024)(128)(4,1)}), s8[4194304]{0:T(1024)(128)(4,1)S(1)}, s32[]{:S(2)}) async-start(s8[16777216]{0:T(1024)(128)(4,1)} %bitcast.478), calls=%async_computation.10 | async-start | bytes 8388608
  483.2 199.3 %reduce-scatter.2.cloned.1.call-start = ((), (), s32[]{:S(2)}) async-start(), calls=%async_computation.5 | async-start | bytes 5308416 | tf_op jit(solution)/shard_map/reduce_scatter | solution.py:834
  495.6 7.7 %copy-start.19 = (bf16[1024,1024]{0,1:T(8,128)(2,1)S(1)}, bf16[1024,1024]{0,1:T(8,128)(2,1)}, u32[]{:S(2)}) copy-start(bf16[1024,1024]{0,1:T(8,128)(2,1)} %get-tuple-element.239) | copy-start | bytes 6291460
  514.0 54.9 %copy-start.5 = (bf16[1024,1024]{0,1:T(8,128)(2,1)S(1)}, bf16[1024,1024]{0,1:T(8,128)(2,1)}, u32[]{:S(2)}) copy-start(bf16[1024,1024]{0,1:T(8,128)(2,1)} %copy-done.4) | copy-start | bytes 6291460
  516.4 57.3 %copy-start.109 = (f32[1024]{0:T(1024)S(1)}, f32[1024]{0:T(1024)}, u32[]{:S(2)}) copy-start(f32[1024]{0:T(1024)} %copy-done.108) | copy-start | bytes 12292
  516.4 57.3 %copy-start.107 = (f32[1024]{0:T(1024)S(1)}, f32[1024]{0:T(1024)}, u32[]{:S(2)}) copy-start(f32[1024]{0:T(1024)} %copy-done.106) | copy-start | bytes 12292
  591.4 95.7 %copy-start.121 = (f32[4]{0:T(128)S(1)}, f32[4]{0:T(128)}, u32[]{:S(2)}) copy-start(f32[4]{0:T(128)} %get-tuple-element.194) | copy-start | bytes 52
  591.4 108.3 %copy-start.117 = (f32[4,4]{1,0:T(4,128)S(1)}, f32[4,4]{1,0:T(4,128)}, u32[]{:S(2)}) copy-start(f32[4,4]{1,0:T(4,128)} %param.37) | copy-start | bytes 196
  668.0 31.7 %copy-start.67 = (f32[8,96,96]{2,1,0:T(8,128)S(1)}, f32[8,96,96]{2,1,0:T(8,128)}, u32[]{:S(2)}) copy-start(f32[8,96,96]{2,1,0:T(8,128)} %get-tuple-element.83) | copy-start | bytes 884740
  680.6 24.1 %copy-start.53 = (f32[4,128,256]{2,1,0:T(8,128)S(1)}, f32[4,128,256]{2,1,0:T(8,128)}, u32[]{:S(2)}) copy-start(f32[4,128,256]{2,1,0:T(8,128)} %get-tuple-element.79) | copy-start | bytes 1572868
  (101 other events, 402.9 us)
Sparse Core Ops, SparseCore 0:
  157.1 84.0 all-reduce.8
  275.2 85.6 all-reduce.12
  363.3 51.5 all-reduce.10
  483.3 85.5 all-reduce.14
Sparse Core Ops, SparseCore 1:
  166.9 78.4 all-gather.2
  495.7 95.3 reduce-scatter.1

commit v2 on v1

--- a/solution.py
+++ b/solution.py
@@ -626,154 +626,646 @@
     )(values)
 
 
-def rms_scale(values, scales):
-    return values * lax.rsqrt(jnp.mean(values * values, axis=-1, keepdims=True) + EPSILON) * scales
-
-
-def geglu_gate(hidden):
-    return hidden[:, 0] * jax.nn.gelu(hidden[:, 1], approximate=False)
-
-
-def cosine(queries, key_rows, head_scale):
-    query_unit = (
-        queries
-        * lax.rsqrt(jnp.sum(queries * queries, axis=-1, keepdims=True) + EPSILON)
-        * head_scale[None, :, None]
-    )
-    key_unit = key_rows * lax.rsqrt(jnp.sum(key_rows * key_rows, axis=-1, keepdims=True) + EPSILON)
-    return (query_unit, key_unit)
+class Ranks:
+    def __init__(self, n_mp):
+        self.d, self.m = lax.axis_index("dp"), lax.axis_index("mp")
+        self.n_x = n_mp // 2
+        self.x, self.c = lax.div(self.m, 2), lax.rem(self.m, 2)
+        self.sibling = (self.d, self.x * 2 + 1 - self.c)
+
+    def rank(self, kx, same):
+        core = jnp.where(same == 1, self.c, 1 - self.c)
+        return lax.rem(self.x + kx, self.n_x) * 2 + core
+
+    def chip(self, kx):
+        return (self.d, lax.rem(self.x + kx, self.n_x) * 2 + self.c)
+
+    def greet(self):
+        greet([(2, lambda k: self.sibling), (self.n_x, self.chip)])
+
+
+class Reduce:
+    def __init__(self, ranks, core_send, core_recv, x_send, x_recv, sems):
+        self.r = ranks
+        self.core_send, self.core_recv, self.x_send, self.x_recv = core_send, core_recv, x_send, x_recv
+        self.sems = sems
+
+    def core_copy(self, kx):
+        return pltpu.make_async_remote_copy(
+            src_ref=self.core_send.at[kx], dst_ref=self.core_recv.at[kx], send_sem=self.sems.at[0, kx],
+            recv_sem=self.sems.at[1, kx], device_id=self.r.sibling, device_id_type=MESH)
+
+    def x_copy(self, kx):
+        return pltpu.make_async_remote_copy(
+            src_ref=self.x_send.at[kx], dst_ref=self.x_recv.at[kx], send_sem=self.sems.at[2, kx],
+            recv_sem=self.sems.at[3, kx], device_id=self.r.chip(kx), device_id_type=MESH)
+
+    def other(self, kx, part):
+        self.core_send[kx] = part.astype(BF16)
+        self.core_copy(kx).start()
+
+    def same(self, kx, part):
+        self.core_copy(kx).wait_recv()
+        self.x_send[kx] = (part + self.core_recv[kx].astype(F32)).astype(BF16)
+        self.x_copy(kx).start()
+
+    def finish(self, part):
+        self.core_copy(0).wait_recv()
+        total = part + self.core_recv[0].astype(F32)
+        for kx in range(1, self.r.n_x):
+            self.x_copy(kx).wait_recv()
+            total = total + self.x_recv[kx].astype(F32)
+        return total
+
+    def drain(self):
+        self.core_copy(0).wait_send()
+        for kx in range(1, self.r.n_x):
+            self.core_copy(kx).wait_send()
+            self.x_copy(kx).wait_send()
+
+
+def reduce_scratch(n_mp, rows):
+    slots = pltpu.VMEM((n_mp // 2, rows, D), BF16)
+    return [slots, slots, slots, slots, pltpu.SemaphoreType.DMA((4, n_mp // 2))]
+
+
+class Gather:
+    def __init__(self, ranks, rows, buffer, sems):
+        self.r, self.rows, self.buffer, self.sems = ranks, rows, buffer, sems
+
+    def at(self, rank):
+        return self.buffer.at[pl.ds(pl.multiple_of(rank * self.rows, self.rows), self.rows), :]
+
+    def x_copy(self, kx, slot):
+        return pltpu.make_async_remote_copy(
+            src_ref=self.at(self.r.m), dst_ref=self.at(slot), send_sem=self.sems.at[0, kx],
+            recv_sem=self.sems.at[1, kx], device_id=self.r.chip(kx), device_id_type=MESH)
+
+    def core_copy(self, kx, out_slot, in_slot):
+        return pltpu.make_async_remote_copy(
+            src_ref=self.at(out_slot), dst_ref=self.at(in_slot), send_sem=self.sems.at[2, kx],
+            recv_sem=self.sems.at[3, kx], device_id=self.r.sibling, device_id_type=MESH)
+
+    def start(self):
+        for kx in range(1, self.r.n_x):
+            self.x_copy(kx, self.r.m).start()
+        self.core_copy(0, self.r.m, self.r.m).start()
+
+    def from_chip(self, kx):
+        return lax.rem(self.r.x + self.r.n_x - kx, self.r.n_x) * 2 + self.r.c
+
+    def from_core(self, kx):
+        return lax.rem(self.r.x + self.r.n_x - kx, self.r.n_x) * 2 + 1 - self.r.c
+
+    def forward(self, kx):
+        slot = self.from_chip(kx)
+        self.x_copy(kx, slot).wait_recv()
+        self.core_copy(kx, slot, slot).start()
+
+    def arrived(self, kx):
+        self.core_copy(kx, self.r.m, self.from_core(kx)).wait_recv()
+
+    def drain(self):
+        for kx in range(1, self.r.n_x):
+            self.x_copy(kx, self.r.m).wait_send()
+        for kx in range(self.r.n_x):
+            self.core_copy(kx, self.r.m, self.r.m).wait_send()
+
+
+def gather_sems(n_mp):
+    return pltpu.SemaphoreType.DMA((4, n_mp // 2))
+
+
+def head_sums(values, ones):
+    return two_part_left(dot_nn, values, ones)
+
+
+def row_sums_factor(values):
+    return lax.rsqrt(jnp.mean(values * values, axis=-1, keepdims=True) + EPSILON)
+
+
+def image_scale(info_ref, mods_ref, which, image):
+    is_long = info_ref[0]
+    row = mods_ref[which, pl.ds(image, 1), :]
+    return 1.0 + (is_long * mods_ref[which, 0:1, :] + (1.0 - is_long) * row)
+
+
+def column_bias(info_ref, image, columns_shape, short):
+    keys = lax.broadcasted_iota(jnp.int32, columns_shape, 0)
+    own = (keys >= image * short) & (keys < (image + 1) * short)
+    return jnp.where(own, 0.0, info_ref[1])
+
+
+SHORT = 256
+
+
+def attn_forward_kernel(
+    n_mp, heads, info_ref, x_ref, mods_ref, scale_ref, ones_ref, wg_ref,
+    q_ref, k_ref, v_ref, normed_ref, att_ref, stats_ref, mid_ref, nm_ref,
+    qu_s, ku_s, vt_s, part_s, core_send, core_recv, x_send, x_recv, sems,
+):
+    r = Ranks(n_mp)
+    tokens = x_ref.shape[0]
+    rows = tokens // n_mp
+    width = q_ref.shape[1]
+    size = width // heads
+    r.greet()
+    red = Reduce(r, core_send, core_recv, x_send, x_recv, sems)
+    at = lambda b: pl.ds(pl.multiple_of(b * rows, rows), rows)
+    image_of = lambda b: lax.div(b * rows, SHORT)
+
+    def project(b, carry):
+        xb = x_ref[at(b), :].astype(F32)
+        normed = (xb * row_sums_factor(xb) * image_scale(info_ref, mods_ref, 0, image_of(b))).astype(BF16)
+        normed_ref[at(b), :] = normed
+        q = dot_nn(normed, wg_ref[0])
+        q_ref[at(b), :] = q
+        qu_s[at(b), :] = (q * lax.rsqrt(head_sums(q * q, ones_ref[...]) + EPSILON) * scale_ref[...]).astype(BF16)
+        k = dot_nn(normed, wg_ref[1])
+        k_ref[at(b), :] = k
+        ku_s[at(b), :] = (k * lax.rsqrt(head_sums(k * k, ones_ref[...]) + EPSILON)).astype(BF16)
+        v = dot_nn(normed, wg_ref[2])
+        v_ref[at(b), :] = v.astype(BF16)
+        vt_s[:, at(b)] = v.T.astype(BF16)
+        return carry
+
+    lax.fori_loop(0, n_mp, project, 0)
+    lanes = lax.broadcasted_iota(jnp.int32, (1, width), 1)
+
+    def block(j, carry):
+        kx, same = lax.rem(1 + lax.div(j, 2), r.n_x), lax.rem(j, 2)
+        b = r.rank(kx, same)
+        bias = column_bias(info_ref, image_of(b), (tokens, 1), SHORT)
+        qu = qu_s[at(b), :]
+        outs = []
+        for h in range(heads):
+            mask = ((lanes >= h * size) & (lanes < (h + 1) * size)).astype(F32).astype(BF16)
+            scores = dot_nt(ku_s[...], qu * mask) + bias
+            top = jnp.max(scores, axis=0, keepdims=True)
+            expon = jnp.exp(scores - top)
+            total = jnp.sum(expon, axis=0, keepdims=True)
+            stats_ref[h : h + 1, at(b)] = top + jnp.log(total)
+            outs.append(dot_nn(vt_s[h * size : (h + 1) * size, :], expon.astype(BF16)) / total)
+        att = jnp.concatenate(outs, axis=0).T.astype(BF16)
+        att_ref[at(b), :] = att
+        part_s[...] = dot_nt(att, wg_ref[3])
+
+        @pl.when(same == 0)
+        def _():
+            red.other(kx, part_s[...])
+
+        @pl.when((same == 1) & (kx > 0))
+        def _():
+            red.same(kx, part_s[...])
+
+        return carry
+
+    lax.fori_loop(0, n_mp, block, 0)
+    if heads < 8:
+        stats_ref[heads:8, :] = jnp.zeros((8 - heads, tokens), F32)
+    middle = x_ref[at(r.m), :].astype(F32) + red.finish(part_s[...])
+    mid_ref[...] = middle
+    nm_ref[...] = (middle * row_sums_factor(middle) * image_scale(info_ref, mods_ref, 1, image_of(r.m))).astype(BF16)
+    red.drain()
+
+
+SMEM_SPEC = pl.BlockSpec(memory_space=pltpu.SMEM)
+
+
+def attn_forward(n_mp, heads, info, x, mods, scale, ones, wg):
+    tokens = x.shape[0]
+    width = wg.shape[2]
+    rows = tokens // n_mp
+    shape = jax.ShapeDtypeStruct
+    return pl.pallas_call(
+        functools.partial(attn_forward_kernel, n_mp, heads),
+        out_shape=(
+            shape((tokens, width), F32),
+            shape((tokens, width), F32),
+            shape((tokens, width), BF16),
+            shape((tokens, D), BF16),
+            shape((tokens, width), BF16),
+            shape((8, tokens), F32),
+            shape((rows, D), F32),
+            shape((rows, D), BF16),
+        ),
+        in_specs=[SMEM_SPEC] + vmem_specs(5),
+        out_specs=tuple(vmem_specs(8)),
+        scratch_shapes=[
+            pltpu.VMEM((tokens, width), BF16),
+            pltpu.VMEM((tokens, width), BF16),
+            pltpu.VMEM((width, tokens), BF16),
+            pltpu.VMEM((rows, D), F32),
+        ]
+        + reduce_scratch(n_mp, rows),
+        compiler_params=pltpu.CompilerParams(
+            collective_id=3, has_side_effects=True, vmem_limit_bytes=VMEM_BYTES
+        ),
+        name="attn_forward",
+    )(info, x, mods, scale, ones, wg)
+
+
+def ffn_kernel(
+    n_dp, n_mp, info_ref, nm_ref, cot_ref, mods_ref, mid_ref, wf_ref,
+    gw_ref, dmid_ref, out_ref, fmod_ref,
+    w_s, nm_s, gated_s, gate_s, slope_s, dh_s, dz_s, part_s, ff_s, w_sem, gather_sem,
+    f_core_send, f_core_recv, f_x_send, f_x_recv, f_sems,
+    b_core_send, b_core_recv, b_x_send, b_x_recv, b_sems,
+):
+    r = Ranks(n_mp)
+    rows = nm_ref.shape[0]
+    tokens = rows * n_mp
+    shard = D // n_dp
+    at = lambda b: pl.ds(pl.multiple_of(b * rows, rows), rows)
+    image_of = lambda b: lax.div(b * rows, SHORT)
+
+    def w_copy(dd, c):
+        return pltpu.make_async_copy(
+            wf_ref.at[dd, pl.ds(c * shard, shard), :],
+            w_s.at[c, pl.ds(pl.multiple_of(dd * shard, shard), shard), :],
+            w_sem.at[dd, c],
+        )
+
+    def w_start(dd, carry):
+        for c in range(3):
+            w_copy(dd, c).start()
+        return carry
+
+    def w_wait(dd, carry):
+        for c in range(3):
+            w_copy(dd, c).wait()
+        return carry
+
+    lax.fori_loop(0, n_dp, w_start, 0)
+    r.greet()
+    nm_s[at(r.m), :] = nm_ref[...]
+    gather = Gather(r, rows, nm_s, gather_sem)
+    gather.start()
+    fwd = Reduce(r, f_core_send, f_core_recv, f_x_send, f_x_recv, f_sems)
+    bwd = Reduce(r, b_core_send, b_core_recv, b_x_send, b_x_recv, b_sems)
+    lax.fori_loop(0, n_dp, w_wait, 0)
+
+    def forward(j, carry):
+        kx = lax.div(j, 2)
+        same = jnp.where(kx == 0, 1 - lax.rem(j, 2), lax.rem(j, 2))
+        b = r.rank(kx, same)
+        back_kx = lax.rem(r.n_x - kx, r.n_x)
+
+        @pl.when((same == 0) & (kx > 0))
+        def _():
+            gather.forward(back_kx)
+
+        @pl.when(same == 0)
+        def _():
+            gather.arrived(back_kx)
+
+        nm = nm_s[at(b), :]
+        hidden = dot_nn(nm, w_s[0])
+        gate = dot_nn(nm, w_s[1])
+        value, slope = gelu_parts(gate)
+        gated = (hidden * value).astype(BF16)
+        gated_s[at(b), :] = gated
+        gate_s[at(b), :] = value
+        slope_s[at(b), :] = hidden * slope
+        part_s[...] = dot_nt(gated, w_s[2])
+
+        @pl.when((same == 1) & (kx == 0))
+        def _():
+            ff_s[...] = part_s[...]
+
+        @pl.when(same == 0)
+        def _():
+            fwd.other(kx, part_s[...])
+
+        @pl.when((same == 1) & (kx > 0))
+        def _():
+            fwd.same(kx, part_s[...])
+
+        return carry
+
+    lax.fori_loop(0, n_mp, forward, 0)
+
+    def live_rows(b):
+        position = lax.broadcasted_iota(jnp.int32, (rows, 1), 0) + b * rows
+        return (position.astype(F32) < info_ref[2]).astype(F32)
+
+    def backward(j, carry):
+        kx, same = lax.rem(1 + lax.div(j, 2), r.n_x), lax.rem(j, 2)
+        b = r.rank(kx, same)
+        dz = (cot_ref[at(b), :].astype(F32) * live_rows(b)).astype(BF16)
+        dz_s[at(b), :] = dz
+        d_gated = dot_nn(dz, w_s[2])
+        d_value = (d_gated * gate_s[at(b), :]).astype(BF16)
+        d_gate = (d_gated * slope_s[at(b), :]).astype(BF16)
+        dh_s[0, at(b), :] = d_value
+        dh_s[1, at(b), :] = d_gate
+        part_s[...] = dot_nt(d_value, w_s[0]) + dot_nt(d_gate, w_s[1])
+
+        @pl.when(same == 0)
+        def _():
+            bwd.other(kx, part_s[...])
+
+        @pl.when((same == 1) & (kx > 0))
+        def _():
+            bwd.same(kx, part_s[...])
+
+        return carry
+
+    lax.fori_loop(0, n_mp, backward, 0)
+
+    step = 512
+
+    def weights(i, carry):
+        cols = pl.ds(pl.multiple_of(i * step, step), step)
+        for c in range(3):
+            left = nm_s[:, cols] if c < 2 else dz_s[:, cols]
+            right = dh_s[c] if c < 2 else gated_s[...]
+            value = dot_tn(left, right).astype(BF16)
+            for s in range(step // shard):
+                gw_ref[i * (step // shard) + s, c * shard : (c + 1) * shard, :] = value[
+                    s * shard : (s + 1) * shard
+                ]
+        return carry
+
+    lax.fori_loop(0, D // step, weights, 0)
+
+    d_nm = bwd.finish(part_s[...])
+    middle = mid_ref[...]
+    live = live_rows(r.m)
+    scale = image_scale(info_ref, mods_ref, 1, image_of(r.m))
+    factor = row_sums_factor(middle)
+    inner = jnp.mean(middle * scale * d_nm, axis=-1, keepdims=True)
+    dmid_ref[...] = cot_ref[at(r.m), :].astype(F32) * live + (
+        factor * scale * d_nm - middle * (factor * factor * factor * inner)
+    )
+    fmod_ref[...] = jnp.sum(d_nm * middle * factor, axis=0, keepdims=True)
+    out_ref[...] = ((middle + fwd.finish(ff_s[...])) * live).astype(BF16)
+    gather.drain()
+    fwd.drain()
+    bwd.drain()
+
+
+def ffn(n_dp, n_mp, info, nm, cot, mods, mid, wf):
+    rows = nm.shape[0]
+    tokens = rows * n_mp
+    units = wf.shape[2]
+    shape = jax.ShapeDtypeStruct
+    return pl.pallas_call(
+        functools.partial(ffn_kernel, n_dp, n_mp),
+        out_shape=(
+            shape(wf.shape, BF16),
+            shape((rows, D), F32),
+            shape((rows, D), BF16),
+            shape((1, D), F32),
+        ),
+        in_specs=[SMEM_SPEC] + vmem_specs(4) + [pl.BlockSpec(memory_space=pl.ANY)],
+        out_specs=tuple(vmem_specs(4)),
+        scratch_shapes=[
+            pltpu.VMEM((3, D, units), BF16),
+            pltpu.VMEM((tokens, D), BF16),
+            pltpu.VMEM((tokens, units), BF16),
+            pltpu.VMEM((tokens, units), F32),
+            pltpu.VMEM((tokens, units), F32),
+            pltpu.VMEM((2, tokens, units), BF16),
+            pltpu.VMEM((tokens, D), BF16),
+            pltpu.VMEM((rows, D), F32),
+            pltpu.VMEM((rows, D), F32),
+            pltpu.SemaphoreType.DMA((n_dp, 3)),
+            gather_sems(n_mp),
+        ]
+        + reduce_scratch(n_mp, rows)
+        + reduce_scratch(n_mp, rows),
+        compiler_params=pltpu.CompilerParams(
+            collective_id=4, has_side_effects=True, vmem_limit_bytes=VMEM_BYTES
+        ),
+        name="ffn",
+    )(info, nm, cot, mods, mid, wf)
+
+
+def attn_backward_kernel(
+    n_mp, heads, info_ref, dmid_ref, x_ref, mods_ref, scale_ref, ones_ref, wg_ref,
+    q_ref, k_ref, v_ref, normed_ref, att_ref, stats_ref,
+    gw_ref, gin_ref, amod_ref, gscale_ref,
+    qu_s, ku_s, kt_s, dy_s, dq_s, dk_s, dv_s, low_s, part_s, gather_sem,
+    core_send, core_recv, x_send, x_recv, sems,
+):
+    r = Ranks(n_mp)
+    rows = dmid_ref.shape[0]
+    tokens = rows * n_mp
+    width = q_ref.shape[1]
+    size = width // heads
+    at = lambda b: pl.ds(pl.multiple_of(b * rows, rows), rows)
+    image_of = lambda b: lax.div(b * rows, SHORT)
+    dy_s[at(r.m), :] = dmid_ref[...].astype(BF16)
+    r.greet()
+    gather = Gather(r, rows, dy_s, gather_sem)
+    gather.start()
+    red = Reduce(r, core_send, core_recv, x_send, x_recv, sems)
+
+    def units(b, carry):
+        q, k = q_ref[at(b), :], k_ref[at(b), :]
+        qu_s[at(b), :] = (q * lax.rsqrt(head_sums(q * q, ones_ref[...]) + EPSILON) * scale_ref[...]).astype(BF16)
+        k_unit = k * lax.rsqrt(head_sums(k * k, ones_ref[...]) + EPSILON)
+        ku_s[at(b), :] = k_unit.astype(BF16)
+        kt_s[:, at(b)] = k_unit.T.astype(BF16)
+        return carry
+
+    lax.fori_loop(0, n_mp, units, 0)
+    dk_s[...] = jnp.zeros_like(dk_s)
+    dv_s[...] = jnp.zeros_like(dv_s)
+    lanes = lax.broadcasted_iota(jnp.int32, (1, width), 1)
+
+    def block(j, carry):
+        kx = lax.div(j, 2)
+        same = 1 - lax.rem(j, 2)
+        b = r.rank(kx, same)
+        back_kx = lax.rem(r.n_x - kx, r.n_x)
+
+        @pl.when((same == 1) & (kx > 0))
+        def _():
+            gather.forward(back_kx)
+
+        @pl.when(same == 0)
+        def _():
+            gather.arrived(back_kx)
+
+        d_att = dot_nn(dy_s[at(b), :], wg_ref[3]).astype(BF16)
+        bias = column_bias(info_ref, image_of(b), (tokens, 1), SHORT)
+        qu = qu_s[at(b), :]
+        outs = []
+        for h in range(heads):
+            mask = ((lanes >= h * size) & (lanes < (h + 1) * size)).astype(F32).astype(BF16)
+            qh = qu * mask
+            dh = d_att * mask
+            probs = jnp.exp(dot_nt(ku_s[...], qh) + bias - stats_ref[h : h + 1, at(b)])
+            d_probs = dot_nt(v_ref[...], dh)
+            inner = jnp.sum(probs * d_probs, axis=0, keepdims=True)
+            d_scores = (probs * (d_probs - inner)).astype(BF16)
+            dv_s[...] = dv_s[...] + dot_nn(probs.astype(BF16), dh)
+            dk_s[...] = dk_s[...] + dot_nn(d_scores, qh)
+            outs.append(dot_nn(kt_s[h * size : (h + 1) * size, :], d_scores))
+        dq_s[at(b), :] = jnp.concatenate(outs, axis=0).T
+        return carry
+
+    lax.fori_loop(0, n_mp, block, 0)
+
+    def inputs(j, scale_grad):
+        kx, same = lax.rem(1 + lax.div(j, 2), r.n_x), lax.rem(j, 2)
+        b = r.rank(kx, same)
+        q, k = q_ref[at(b), :], k_ref[at(b), :]
+        q_factor = lax.rsqrt(head_sums(q * q, ones_ref[...]) + EPSILON)
+        k_factor = lax.rsqrt(head_sums(k * k, ones_ref[...]) + EPSILON)
+        dqu, dku = dq_s[at(b), :], dk_s[at(b), :]
+        q_unit, k_unit = q * q_factor, k * k_factor
+        q_along = dqu * q_unit
+        d_q = (scale_ref[...] * q_factor * (dqu - q_unit * head_sums(q_along, ones_ref[...]))).astype(BF16)
+        d_k = (k_factor * (dku - k_unit * head_sums(dku * k_unit, ones_ref[...]))).astype(BF16)
+        d_v = dv_s[at(b), :].astype(BF16)
+        low_s[at(b), 0:width] = d_q
+        low_s[at(b), width : 2 * width] = d_k
+        low_s[at(b), 2 * width : 3 * width] = d_v
+        part_s[...] = dot_nt(d_q, wg_ref[0]) + dot_nt(d_k, wg_ref[1]) + dot_nt(d_v, wg_ref[2])
+
+        @pl.when(same == 0)
+        def _():
+            red.other(kx, part_s[...])
+
+        @pl.when((same == 1) & (kx > 0))
+        def _():
+            red.same(kx, part_s[...])
+
+        return scale_grad + jnp.sum(q_along, axis=0, keepdims=True)
+
+    gscale_ref[...] = lax.fori_loop(0, n_mp, inputs, jnp.zeros((1, width), F32))
+
+    step = 512
+
+    def weights(i, carry):
+        cols = pl.ds(pl.multiple_of(i * step, step), step)
+        value = dot_tn(normed_ref[:, cols], low_s[...]).astype(BF16)
+        for c in range(3):
+            gw_ref[c, cols, :] = value[:, c * width : (c + 1) * width]
+        gw_ref[3, cols, :] = dot_tn(dy_s[:, cols], att_ref[...]).astype(BF16)
+        return carry
+
+    lax.fori_loop(0, D // step, weights, 0)
+
+    d_normed = red.finish(part_s[...])
+    x = x_ref[at(r.m), :].astype(F32)
+    scale = image_scale(info_ref, mods_ref, 0, image_of(r.m))
+    factor = row_sums_factor(x)
+    inner = jnp.mean(x * scale * d_normed, axis=-1, keepdims=True)
+    gin_ref[...] = dmid_ref[...] + (factor * scale * d_normed - x * (factor * factor * factor * inner))
+    amod_ref[...] = jnp.sum(d_normed * x * factor, axis=0, keepdims=True)
+    gather.drain()
+    red.drain()
+
+
+def attn_backward(n_mp, heads, info, dmid, x, mods, scale, ones, wg, q, k, v, normed, att, stats):
+    rows = dmid.shape[0]
+    tokens = rows * n_mp
+    width = q.shape[1]
+    shape = jax.ShapeDtypeStruct
+    return pl.pallas_call(
+        functools.partial(attn_backward_kernel, n_mp, heads),
+        out_shape=(
+            shape(wg.shape, BF16),
+            shape((rows, D), F32),
+            shape((1, D), F32),
+            shape((1, width), F32),
+        ),
+        in_specs=[SMEM_SPEC] + vmem_specs(12),
+        out_specs=tuple(vmem_specs(4)),
+        scratch_shapes=[
+            pltpu.VMEM((tokens, width), BF16),
+            pltpu.VMEM((tokens, width), BF16),
+            pltpu.VMEM((width, tokens), BF16),
+            pltpu.VMEM((tokens, D), BF16),
+            pltpu.VMEM((tokens, width), F32),
+            pltpu.VMEM((tokens, width), F32),
+            pltpu.VMEM((tokens, width), F32),
+            pltpu.VMEM((tokens, 3 * width), BF16),
+            pltpu.VMEM((rows, D), F32),
+            gather_sems(n_mp),
+        ]
+        + reduce_scratch(n_mp, rows),
+        compiler_params=pltpu.CompilerParams(
+            collective_id=5, has_side_effects=True, vmem_limit_bytes=VMEM_BYTES
+        ),
+        name="attn_backward",
+    )(info, dmid, x, mods, scale, ones, wg, q, k, v, normed, att, stats)
+
+
+def spread_kernel(n_mp, out_ref, gin_ref, out_all, gin_all, gin_s, out_sem, gin_sem):
+    r = Ranks(n_mp)
+    rows = out_ref.shape[0]
+    at = lambda b: pl.ds(pl.multiple_of(b * rows, rows), rows)
+    r.greet()
+    out_all[at(r.m), :] = out_ref[...]
+    gin_s[at(r.m), :] = gin_ref[...].astype(BF16)
+    one = Gather(r, rows, out_all, out_sem)
+    two = Gather(r, rows, gin_s, gin_sem)
+    one.start()
+    two.start()
+    gin_all[at(r.m), :] = gin_ref[...]
+    for kx in range(1, r.n_x):
+        one.forward(kx)
+        two.forward(kx)
+        gin_all[at(two.from_chip(kx)), :] = gin_s[at(two.from_chip(kx)), :].astype(F32)
+    for kx in range(r.n_x):
+        one.arrived(kx)
+        two.arrived(kx)
+        gin_all[at(two.from_core(kx)), :] = gin_s[at(two.from_core(kx)), :].astype(F32)
+    one.drain()
+    two.drain()
+
+
+def spread(n_mp, out, gin):
+    rows = out.shape[0]
+    tokens = rows * n_mp
+    return pl.pallas_call(
+        functools.partial(spread_kernel, n_mp),
+        out_shape=(
+            jax.ShapeDtypeStruct((tokens, D), BF16),
+            jax.ShapeDtypeStruct((tokens, D), F32),
+        ),
+        in_specs=vmem_specs(2),
+        out_specs=tuple(vmem_specs(2)),
+        scratch_shapes=[pltpu.VMEM((tokens, D), BF16), gather_sems(n_mp), gather_sems(n_mp)],
+        compiler_params=pltpu.CompilerParams(
+            collective_id=6, has_side_effects=True, vmem_limit_bytes=VMEM_BYTES
+        ),
+        name="spread",
+    )(out, gin)
 
 
 def middle_part(block_input, out_cotangent, mods, my_lengths, wg, wf, head_scale):
-    n_dp = lax.axis_size("dp")
-    w_in = jnp.transpose(wg[:3], (1, 0, 2))
-    w_out = wg[3].T
-    rows = D // n_dp
-    w_up = jnp.transpose(wf.reshape(n_dp, 3, rows, -1)[:, :2], (0, 2, 1, 3)).reshape(D, 2, -1)
-    w_down = wf.reshape(n_dp, 3, rows, -1)[:, 2].reshape(D, -1).T
-    slot_count = block_input.shape[0]
-    image_ends = jnp.cumsum(my_lengths)
-    position = jnp.arange(slot_count, dtype=jnp.int32)
-    slot_of = jnp.sum((position[:, None] >= image_ends[None, :]).astype(jnp.int32), axis=1)
-    live_rows = (position < image_ends[-1]).astype(jnp.float32)[:, None]
-    member = (slot_of[:, None] == jnp.arange(IMG_DEV, dtype=jnp.int32)[None, :]).astype(jnp.float32)
-    same_image = slot_of[:, None] == slot_of[None, :]
-    hi = lax.Precision.HIGHEST
-    attn_mod = 1.0 + jnp.dot(member, mods[0], precision=hi)
-    ff_mod = 1.0 + jnp.dot(member, mods[1], precision=hi)
-    heads_here = head_scale.shape[0]
-    width_here = w_in.shape[2]
-    head_size = width_here // heads_here
-    inputs = block_input.astype(jnp.float32)
-    normed_in, in_back = jax.vjp(rms_scale, inputs, attn_mod)
-    low_in = normed_in.astype(jnp.bfloat16)
-    projected = jnp.einsum("td,dcf->tcf", low_in, w_in, preferred_element_type=jnp.float32)
-    queries = projected[:, 0].reshape(slot_count, heads_here, head_size)
-    key_rows = projected[:, 1].reshape(slot_count, heads_here, head_size)
-    (query_unit, key_unit), cosine_back = jax.vjp(cosine, queries, key_rows, head_scale)
-    query_low = query_unit.astype(jnp.bfloat16)
-    key_low = key_unit.astype(jnp.bfloat16)
-    value_low = projected[:, 2].reshape(slot_count, heads_here, head_size).astype(jnp.bfloat16)
-    scores = jnp.einsum("thd,uhd->htu", query_low, key_low, preferred_element_type=jnp.float32)
-    scores = jnp.where(same_image[None], scores, MASKED)
-    row_max = jnp.max(scores, axis=-1, keepdims=True)
-    expon = jnp.exp(scores - row_max)
-    row_total = jnp.sum(expon, axis=-1, keepdims=True)
-    probabilities = expon / row_total
-    log_total = row_max + jnp.log(row_total)
-    attended = jnp.einsum(
-        "htu,uhd->thd",
-        probabilities.astype(jnp.bfloat16),
-        value_low,
-        preferred_element_type=jnp.float32,
-    )
-    attended_low = attended.reshape(slot_count, width_here).astype(jnp.bfloat16)
-    branch_attn = lax.psum(jnp.dot(attended_low, w_out, preferred_element_type=jnp.float32), "mp")
-    middle = inputs + branch_attn
-    normed_mid, mid_back = jax.vjp(rms_scale, middle, ff_mod)
-    low_mid = normed_mid.astype(jnp.bfloat16)
-    hidden = jnp.einsum("td,dcf->tcf", low_mid, w_up, preferred_element_type=jnp.float32)
-    gated_vals, gate_back = jax.vjp(geglu_gate, hidden)
-    gated_low = gated_vals.astype(jnp.bfloat16)
-    branch_ff = lax.psum(
-        jnp.dot(gated_low, w_down, preferred_element_type=jnp.float32).astype(jnp.bfloat16), "mp"
-    ).astype(jnp.float32)
-    layer_out = (live_rows * (middle + branch_ff)).astype(jnp.bfloat16)
-    out_grad = live_rows * out_cotangent.astype(jnp.float32)
-    grad_branch = out_grad.astype(jnp.bfloat16)
-    grad_downproj = jnp.dot(gated_low.T, grad_branch, preferred_element_type=jnp.float32)
-    grad_gated = jnp.dot(grad_branch, w_down.T, preferred_element_type=jnp.float32)
-    (grad_hidden,) = gate_back(grad_gated)
-    grad_hidden_low = grad_hidden.astype(jnp.bfloat16)
-    grad_upproj = jnp.einsum(
-        "td,tcf->dcf", low_mid, grad_hidden_low, preferred_element_type=jnp.float32
-    )
-    grad_low_mid = lax.psum(
-        jnp.einsum("tcf,dcf->td", grad_hidden_low, w_up, preferred_element_type=jnp.float32), "mp"
-    )
-    grad_mid_norm, grad_ff_mod = mid_back(grad_low_mid)
-    grad_middle = out_grad + grad_mid_norm
-    grad_y = grad_middle.astype(jnp.bfloat16)
-    grad_outproj = jnp.dot(attended_low.T, grad_y, preferred_element_type=jnp.float32)
-    grad_att = (
-        jnp.dot(grad_y, w_out.T, preferred_element_type=jnp.float32)
-        .astype(jnp.bfloat16)
-        .reshape(slot_count, heads_here, head_size)
-    )
-    again = jnp.einsum("thd,uhd->htu", query_low, key_low, preferred_element_type=jnp.float32)
-    again = jnp.where(same_image[None], again, MASKED)
-    probs_again = jnp.exp(again - log_total)
-    grad_values = jnp.einsum(
-        "htu,thd->uhd",
-        probs_again.astype(jnp.bfloat16),
-        grad_att,
-        preferred_element_type=jnp.float32,
-    )
-    grad_probs = jnp.einsum("thd,uhd->htu", grad_att, value_low, preferred_element_type=jnp.float32)
-    inner = jnp.sum(grad_probs * probs_again, axis=-1, keepdims=True)
-    grad_scores = (probs_again * (grad_probs - inner)).astype(jnp.bfloat16)
-    grad_qunit = jnp.einsum(
-        "htu,uhd->thd", grad_scores, key_low, preferred_element_type=jnp.float32
-    )
-    grad_kunit = jnp.einsum(
-        "htu,thd->uhd", grad_scores, query_low, preferred_element_type=jnp.float32
-    )
-    grad_queries, grad_keys, grad_headscale = cosine_back((grad_qunit, grad_kunit))
-    grad_projected = jnp.stack(
-        [
-            grad_queries.reshape(slot_count, width_here),
-            grad_keys.reshape(slot_count, width_here),
-            grad_values.reshape(slot_count, width_here),
-        ],
-        axis=1,
-    ).astype(jnp.bfloat16)
-    grad_inproj = jnp.einsum(
-        "td,tcf->dcf", low_in, grad_projected, preferred_element_type=jnp.float32
-    )
-    grad_low_in = lax.psum(
-        jnp.einsum("tcf,dcf->td", grad_projected, w_in, preferred_element_type=jnp.float32), "mp"
-    )
-    grad_in_norm, grad_attn_mod = in_back(grad_low_in)
-    input_grad = grad_middle + grad_in_norm
-    grad_mods = jnp.stack(
-        [
-            jnp.dot(member.T, grad_attn_mod, precision=hi),
-            jnp.dot(member.T, grad_ff_mod, precision=hi),
-        ],
-        axis=0,
-    ) / lax.axis_size("mp")
-    grad_attn_w = jnp.concatenate(
-        [jnp.transpose(grad_inproj, (1, 0, 2)), grad_outproj.T[None]], axis=0
-    ).astype(BF16)
-    grad_ffn_w = jnp.concatenate(
-        [
-            jnp.transpose(grad_upproj, (1, 0, 2)).reshape(2, n_dp, rows, -1),
-            grad_downproj.T.reshape(1, n_dp, rows, -1),
-        ],
-        axis=0,
-    ).astype(BF16)
-    grad_ffn_w = jnp.transpose(grad_ffn_w, (1, 0, 2, 3)).reshape(n_dp, 3 * rows, -1)
-    return layer_out, input_grad, grad_mods, grad_attn_w, grad_ffn_w, grad_headscale
+    n_dp, n_mp = lax.axis_size("dp"), lax.axis_size("mp")
+    m = lax.axis_index("mp")
+    tokens = block_input.shape[0]
+    rows = tokens // n_mp
+    heads = head_scale.shape[0]
+    width = wg.shape[2]
+    size = width // heads
+    is_long = (my_lengths[0] > SHORT).astype(F32)
+    live = jnp.sum(my_lengths).astype(F32)
+    info = jnp.stack([is_long, (1.0 - is_long) * MASKED, live, live])
+    scale = jnp.repeat(head_scale, size)[None, :]
+    group = jnp.arange(width, dtype=jnp.int32) // size
+    ones = (group[:, None] == group[None, :]).astype(BF16)
+    q, k, v, normed, att, stats, mid, nm = attn_forward(
+        n_mp, heads, info, block_input, mods, scale, ones, wg
+    )
+    gw_ffn, dmid, out_own, fmod = ffn(n_dp, n_mp, info, nm, out_cotangent, mods, mid, wf)
+    gw_attn, gin_own, amod, gscale = attn_backward(
+        n_mp, heads, info, dmid, block_input, mods, scale, ones, wg, q, k, v, normed, att, stats
+    )
+    layer_out, input_grad = spread(n_mp, out_own, gin_own)
+    image = jnp.where(is_long > 0, 0, m * rows // SHORT)
+    chosen = (jnp.arange(IMG_DEV, dtype=jnp.int32) == image).astype(F32)
+    grad_mods = chosen[None, :, None] * jnp.stack([amod, fmod])
+    grad_headscale = jnp.sum(gscale.reshape(heads, size), axis=1)
+    return layer_out, input_grad, grad_mods, gw_attn, gw_ffn, grad_headscale
 
 
 def per_device(

time: 769 us -> 486 us (0.63)
  waiting for transfers between devices: 234 us -> 0.06 us
  Pallas kernels: 167 us -> 353 us
  matrix products: 105 us -> 1.83 us
  other arithmetic: 128 us -> 45.2 us
  local copies, waits for them, and re-layouts: 101 us -> 58.7 us
    psum x4 -> x0, waiting for transfers between devices: 234 us -> none  [the longest x1 72.3 us: middle_part(): lax.psum(jnp.einsum('tcf,dcf->td', grad_hidden_low, w_up, preferred_eleme...]
    pallas_call x0 -> x4, Pallas kernels: none -> 156 us  [the longest x1 49.5 us: ffn(): pl.pallas_call(functools.partial(ffn_kernel, n_dp, n_mp), out_shape=(shap...]
    dot_general x22 -> x0, matrix products: 103 us -> none  [the longest x1 15.3 us: middle_part(): jnp.einsum('thd,uhd->htu', grad_att, value_low, preferred_element_type=jn...]
    unnamed x286 -> x130, local copies, waits for them, and re-layouts: 67.6 us -> 36.8 us
    pallas_call x1, Pallas kernels: 81 us -> 109 us  [front(): pl.pallas_call(functools.partial(front_kernel, n_dp, n_mp), out_shape=(ja...]
    convert_element_type x6 -> x2, other arithmetic: 25.7 us -> 0.76 us  [the longest x1 0.76 us: middle_part(): ones = (group[:, None] == group[None, :]).astype(BF16)]
    reduce_sum x8 -> x2, other arithmetic: 23.6 us -> 0.82 us  [the longest x1 0.7 us: middle_part(): live = jnp.sum(my_lengths).astype(F32)]
    add x3 -> x0, other arithmetic: 14 us -> none  [the longest x1 7.78 us: middle_part(): grad_middle = out_grad + grad_mid_norm]
  transfers between devices with their start and end apart: 6 -> 2, of which waited for: 4 -> 0; matrix products, arithmetic and copies ran while one was open for 14% -> 8% of each run, Pallas kernels for 10% -> 61%
where the time goes in v2:
time: 486 us; the launch traced here: 481 us
  Pallas kernels  353 us (73%)
  local copies, waits for them, and re-layouts  58.7 us (12%)
  other arithmetic  45.2 us (9%)
  between operations  21.4 us (4%)
    pallas_call x1, Pallas kernels, front(): pl.pallas_call(functools.partial(front_kernel, n_dp, n_mp), out_shape=(ja...  109 us
    pallas_call x1, Pallas kernels, back(): pl.pallas_call(functools.partial(back_kernel, n_dp, n_mp), out_shape=(sha...  77.6 us
    pallas_call x1, Pallas kernels, ffn(): pl.pallas_call(functools.partial(ffn_kernel, n_dp, n_mp), out_shape=(shap...  49.5 us
    pallas_call x1, Pallas kernels, attn_backward(): pl.pallas_call(functools.partial(attn_backward_kernel, n_mp, heads), out_...  44.3 us
    unnamed x130, local copies, waits for them, and re-layouts  36.8 us
    pallas_call x1, Pallas kernels, attn_forward(): pl.pallas_call(functools.partial(attn_forward_kernel, n_mp, heads), out_s...  31.1 us
    pallas_call x1, Pallas kernels, spread(): pl.pallas_call(functools.partial(spread_kernel, n_mp), out_shape=(jax.Sha...  31.1 us
    another operation x22, other arithmetic, adamw_step(): return (jnp.stack([weight, average]), first, second)  20.9 us
  transfers between devices with their start and end apart: 2, of which 0 were waited for; matrix products, arithmetic and copies ran while one was open for 8% of the time, Pallas kernels for 61%

profile of v2, /device:TPU:0, one launch (start us, length us, event | category | flops | bytes accessed | tf_op | source)
XLA Modules:
  0.0 480.7 jit_solution(17657994900539054510)
XLA Ops:
  7.3 2.3 fusion.92
  9.8 3.9 fusion.90
  16.1 4.2 fusion.89
  21.2 1.5 fusion.91
  30.4 1.6 fusion.50.wmd_ref
  32.0 1.8 fusion.44.ecols_ref
  33.8 109.1 %front.1 = (bf16[4,1024,256]{2,1,0:T(8,128)(2,1)}, f32[2,4,1024]{2,1,0:T(4,128)}, f32[8,40,96]{2,1,0:T(8,128)}, f32[2,4,576]{2,1,0:T(4,128)}, f32[32,576]{1,0:T(8,128)}, /*index=5*/f32[8,32,96]{2,1,0:T(8,128)}) custom-call(bf16[4,128,256]{2,1,0:T(8,128)(2,1)} %pad_maximum_fusion.9.shard_ref, bf16[32,96]{1,0:T(8,128)(2,1)} %fusion.54.feats_ref, ...), custom_call_target="tpu_custom_call" | custom-call | tf_op jit(solution)/shard_map/front/pallas_call | solution.py:324
  144.3 31.1 %attn_forward.1 = (f32[1024,256]{1,0:T(8,128)}, f32[1024,256]{1,0:T(8,128)}, bf16[1024,256]{1,0:T(8,128)(2,1)}, bf16[1024,1024]{1,0:T(8,128)(2,1)}, bf16[1024,25...) custom-call(f32[4]{0:T(128)} %pad_maximum_fusion.13.info_ref, ...), custom_call_target="tpu_custom_call" | custom-call | tf_op jit(solution)/shard_map/attn_forward/pallas_call | solution.py:840
  175.4 49.5 %ffn.1 = (bf16[8,384,768]{2,1,0:T(8,128)(2,1)}, f32[256,1024]{1,0:T(8,128)}, bf16[256,1024]{1,0:T(8,128)(2,1)}, f32[1,1024]{1,0:T(1,128)}) custom-call(f32[4]{0:T(128)} %pad_maximum_fusion.13.info_ref, bf16[256,1024]{1,0:T(8,128)(2,1)} %get-tuple-element.93.nm_ref, bf16[1024,1024]{1,0:T(8,128)(2,1)} %cot_ref.1, f32[2,4,1024]{2,1,0:T(4,128)} %get-tuple-element.91.mods_ref, ...), custom_call_target="tpu_custom_call" | custom-call | tf_op jit(solution)/shard_map/ffn/pallas_call | solution.py:1013
  225.0 2.0 copy.142
  227.0 1.9 copy.143
  232.8 44.3 %attn_backward.1 = (bf16[4,1024,256]{2,1,0:T(8,128)(2,1)}, f32[256,1024]{1,0:T(8,128)}, f32[1,1024]{1,0:T(1,128)}, f32[1,256]{1,0:T(1,128)}) custom-call(f32[4]{0:T(128)} %pad_maximum_fusion.13.info_ref, f32[256,1024]{1,0:T(8,128)} %get-tuple-element.96.dmid_ref, bf16[1024,1024]{1,0:T(8,128)(2,1)} %x_ref.3, f32[2,4,1024]{2,1,0:T(4,128)} %get-tuple-element.91.mods_ref, ...), custom_call_target="tpu_custom_call" | custom-call | tf_op jit(solution)/shard_map/attn_backward/pallas_call | solution.py:1169
  279.1 31.1 %spread.1 = (bf16[1024,1024]{1,0:T(8,128)(2,1)}, f32[1024,1024]{1,0:T(8,128)}) custom-call(bf16[256,1024]{1,0:T(8,128)(2,1)} %get-tuple-element.95.out_ref, f32[256,1024]{1,0:T(8,128)} %get-tuple-element.103.gin_ref), custom_call_target="tpu_custom_call" | custom-call | tf_op jit(solution)/shard_map/spread/pallas_call | solution.py:1226
  310.9 77.6 %back.1 = (f32[4,128,256]{2,1,0:T(8,128)}, f32[2,96,1024]{2,1,0:T(8,128)}, f32[96,576]{1,0:T(8,128)}, f32[2,96,576]{2,1,0:T(8,128)}, f32[8,96,96]{2,1,0:T(8,128)}, /*index=5*/f32[96,1000]{1,0:T(8,128)}, f32[8,96]{1,0:T(8,128)}) custom-call(bf16[4,1024,256]{2,1,0:T(8,128)(2,1)} %get-tuple-element.106.grads_ref, ...), custom_call_target="tpu_custom_call" | custom-call | tf_op jit(solution)/shard_map/back/pallas_call | solution.py:534
  388.6 1.8 multiply_reduce_fusion.5
  390.3 1.9 multiply_reduce_fusion.1
  393.6 1.7 multiply_reduce_fusion.4
  398.0 1.8 multiply_reduce_fusion.3
  400.5 2.0 multiply_reduce_fusion
  405.8 10.7 %norm_all.1 = f32[8,128]{1,0:T(8,128)} custom-call(f32[8,128]{1,0:T(8,128)} %copy-done.39), custom_call_target="tpu_custom_call" | custom-call | tf_op jit(solution)/shard_map/norm_all/pallas_call | solution.py:610
  420.4 2.4 fusion.40
  422.8 2.4 fusion.26
  427.3 3.0 fusion.29
  433.0 2.4 copy.126
  435.3 1.5 copy.127
  438.8 1.7 copy.123
  449.3 2.1 pad_maximum_fusion.4
  451.4 2.3 copy.120
  453.7 1.8 fusion.10
  455.6 2.4 copy.117
  470.0 1.6 copy-done
  471.6 2.0 copy.259
  (189 shorter events, 52.0 us)
Async XLA Ops:
  7.2 168.2 %all-gather.3.cloned.1.call-start = ((), (), s32[]{:S(2)}) async-start(), calls=%async_computation.2 | async-start | bytes 5308416 | tf_op jit(solution)/shard_map/all_gather | solution.py:1303
  14.6 385.9 %reduce-scatter.2.cloned.1.call-start = ((), (), s32[]{:S(2)}) async-start(), calls=%async_computation.1 | async-start | bytes 5308416 | tf_op jit(solution)/shard_map/reduce_scatter | solution.py:1326
  16.1 5.2 %copy-start.13 = (f32[4,96,2,576]{3,2,1,0:T(2,128)S(1)}, f32[4,96,2,576]{3,2,1,0:T(2,128)}, u32[]{:S(2)}) copy-start(f32[4,96,2,576]{3,2,1,0:T(2,128)} %param.33) | copy-start | bytes 5308420
  22.7 3.6 copy-start.41
  22.7 4.9 %copy-start.49 = (f32[32]{0:T(128)S(1)}, f32[32]{0:T(128)}, u32[]{:S(2)}) copy-start(f32[32]{0:T(128)} %param.23) | copy-start | bytes 388
  22.7 4.9 %copy-start.47 = (f32[384]{0:T(512)S(1)}, f32[384]{0:T(512)}, u32[]{:S(2)}) copy-start(f32[384]{0:T(512)} %param.26) | copy-start | bytes 4612
  24.2 7.8 %copy-start.45 = (s32[32]{0:T(128)S(1)}, s32[32]{0:T(128)}, u32[]{:S(2)}) copy-start(s32[32]{0:T(128)} %param.24) | copy-start | bytes 388
  225.0 4.9 %copy-start.38 = (f32[1,256,128]{2,1,0:T(8,128)S(1)}, f32[1,256,128]{2,1,0:T(8,128)}, u32[]{:S(2)}) copy-start(f32[1,256,128]{2,1,0:T(8,128)} %get-tuple-element.253) | copy-start | bytes 393220
  225.0 5.6 %copy-start.37 = (f32[1,256,128]{2,1,0:T(8,128)S(1)}, f32[1,256,128]{2,1,0:T(8,128)}, u32[]{:S(2)}) copy-start(f32[1,256,128]{2,1,0:T(8,128)} %get-tuple-element.252) | copy-start | bytes 393220
  225.0 7.1 %copy-start.46 = (s32[32]{0:T(128)S(1)}, s32[32]{0:T(128)}, u32[]{:S(2)}) copy-start(s32[32]{0:T(128)} %param.24) | copy-start | bytes 388
  277.2 33.1 %copy-start.43 = (f32[1,1024]{1,0:T(1,128)S(1)}, f32[1,1024]{1,0:T(1,128)}, u32[]{:S(2)}) copy-start(f32[1,1024]{1,0:T(1,128)} %get-tuple-element.108) | copy-start | bytes 12292
  277.2 33.1 %copy-start.44 = (f32[1,1024]{1,0:T(1,128)S(1)}, f32[1,1024]{1,0:T(1,128)}, u32[]{:S(2)}) copy-start(f32[1,1024]{1,0:T(1,128)} %get-tuple-element.107) | copy-start | bytes 12292
  388.5 7.4 %copy-start.42 = (f32[8,96]{1,0:T(8,128)S(1)}, f32[8,96]{1,0:T(8,128)}, u32[]{:S(2)}) copy-start(f32[8,96]{1,0:T(8,128)} %get-tuple-element.120) | copy-start | bytes 9220
  388.5 8.8 %copy-start.30 = (f32[96,576]{1,0:T(8,128)S(1)}, f32[96,576]{1,0:T(8,128)}, u32[]{:S(2)}) copy-start(f32[96,576]{1,0:T(8,128)} %get-tuple-element.116) | copy-start | bytes 663556
  388.5 11.2 %copy-start.12 = (f32[4,128,256]{2,1,0:T(8,128)S(1)}, f32[4,128,256]{2,1,0:T(8,128)}, u32[]{:S(2)}) copy-start(f32[4,128,256]{2,1,0:T(8,128)} %get-tuple-element.113) | copy-start | bytes 1572868
  418.4 4.4 copy-start.9
  427.3 4.2 copy-start.4
  427.3 4.2 copy-start.5
  427.3 4.2 copy-start.6
  427.3 4.2 copy-start.7
  438.8 4.0 copy-start.8
  438.8 4.0 copy-start.29
  449.3 4.4 copy-start.1
  449.3 4.4 copy-start.2
  449.3 4.4 copy-start.3
  459.4 4.1 copy-start.33
  460.9 4.2 copy-start.31
  460.9 4.2 copy-start.32
  462.0 3.9 copy-start.22
  462.0 3.9 copy-start.23
  463.7 3.2 copy-start.26
  463.7 3.2 copy-start.27
  (20 other events, 43.7 us)
Sparse Core Ops, SparseCore 0:
  14.7 113.9 all-gather.2
  225.1 95.3 reduce-scatter.1
